TPU v7x, 32 devices: a whole 2x2x4 slice. The times are simulated.
32 devices in a mesh: batch: 8 (over y, x, core), shard: 4 (over z).
Axes of the slice: x: 2, y: 2, z: 4, core: 2. Of those that a mesh axis runs over, the one named last changes fastest.
Arguments:
- inputs: bfloat16 [32, 1024, 512], P(('batch', 'shard')), may hold values from -10 to 10
- cotangent: bfloat16 [32, 1024, 512], P(('batch', 'shard')), may hold values from -6 to 6
- lengths: int32 [32], P(('batch', 'shard')), may hold values from 512 to 1024, as said below
- segment_ids: int32 [32, 1024], P(('batch', 'shard')), may hold values from 0 to 7, never falling along the last dimension, each value on 1 to 512 neighbouring positions
- group_tags: int32 [32, 8], P(('batch', 'shard')), may hold values from 0 to 3
- weights: float32 [512, 6144], P('shard'), may hold values from -2 to 2
- first_moments: float32 [512, 6144], P('shard'), may hold values from -4 to 4
- second_moments: float32 [512, 6144], P('shard'), may hold values from 1 to 4
- vectors: float32 [12, 512], P(None, 'shard'), may hold values from -3 to 3
- vector_first: float32 [12, 512], P(None, 'shard'), may hold values from -16 to 16
- vector_second: float32 [12, 512], P(None, 'shard'), may hold values from 9 to 36
Outputs:
- outputs: bfloat16 [32, 1024, 512], P(('batch', 'shard'))
- input_grad: float32 [32, 1024, 512], P(('batch', 'shard'))
- grad_w: float32 [512, 6144], P('shard')
- grad_v: float32 [12, 512], P(None, 'shard')
- grad_norm: float32 [], replicated
- new_weights: float32 [512, 6144], P('shard')
- new_first: float32 [512, 6144], P('shard')
- new_second: float32 [512, 6144], P('shard')
- new_vectors: float32 [12, 512], P(None, 'shard')
- new_vector_first: float32 [12, 512], P(None, 'shard')
- new_vector_second: float32 [12, 512], P(None, 'shard')
Inputs may be any that keep to these rules, and one draw needn't show every extreme that they name: `lengths`: each row's live tokens; positions at or past it are padding.
All inputs are finite; a program needn't handle non-finite values.
Results may differ from a plain program's by a relative error of at most 0.028.
The roundings to bfloat16 on the way count: a program that leaves them out, or rounds other values in their place, can miss the bound.
Values may be sent and summed in bfloat16 or wider, within the bound.
No kernel may reach another device: no remote copies, remote signals or barrier semaphores. Data moves between devices by JAX's collectives and lax.ppermute only.
A program may use at most 256 MiB of HBM per device.

v0:
```python
import math

import jax
import jax.numpy as jnp
from jax import lax
from jax.sharding import PartitionSpec as P

D = 512
HEADS = 8
STEP = 10
WCOLS = 6144


NORM_EPS = 1e-05
BETA_ONE = 0.5
BETA_TWO = 0.5
ADAM_EPS = 1e-08
DECAY = 0.01
WARMUP = 4000.0
RATE_SCALE = 150000.0


def layer_norm(signal, norm_gain, norm_shift):
    row_mean = jnp.mean(signal, axis=-1, keepdims=True)
    centred = signal - row_mean
    variance = jnp.mean(centred * centred, axis=-1, keepdims=True)
    return centred * lax.rsqrt(variance + NORM_EPS) * norm_gain + norm_shift


def gelu_tanh(signal):
    return (
        0.5
        * signal
        * (1.0 + jnp.tanh(0.7978845608028654 * (signal + 0.044715 * signal * signal * signal)))
    )


def adam_update(master, moment_one, moment_two, gradient):
    moment_one = BETA_ONE * moment_one + (1.0 - BETA_ONE) * gradient
    moment_two = BETA_TWO * moment_two + (1.0 - BETA_TWO) * gradient * gradient
    step_rate = RATE_SCALE * D ** (-0.5) * min(STEP ** (-0.5), STEP * WARMUP ** (-1.5))
    fixed_first = moment_one / (1.0 - BETA_ONE**STEP)
    fixed_second = moment_two / (1.0 - BETA_TWO**STEP)
    master = master - step_rate * (
        fixed_first / (jnp.sqrt(fixed_second) + ADAM_EPS) + DECAY * master
    )
    return (master, moment_one, moment_two)


def group_of(seg_rows, tag_rows):
    tag_count = tag_rows.shape[1]
    matches = seg_rows[:, :, None] == jnp.arange(tag_count, dtype=jnp.int32)[None, None, :]
    return jnp.sum(jnp.where(matches, tag_rows[:, None, :], 0), axis=2)


def block_mask(seg_row, group_row, length, offset, block_size):
    seq_len = seg_row.shape[0]
    seg_query = lax.dynamic_slice_in_dim(seg_row, offset, block_size, 0)
    group_query = lax.dynamic_slice_in_dim(group_row, offset, block_size, 0)
    pos_query = offset + jnp.arange(block_size, dtype=jnp.int32)
    pos_key = jnp.arange(seq_len, dtype=jnp.int32)
    related = (seg_query[:, None] == seg_row[None, :]) | (
        group_query[:, None] == group_row[None, :]
    )
    return related & (pos_key[None, :] < length) | (pos_query[:, None] == pos_key[None, :])


def block_scores(queries, key_rows, seg_row, group_row, length, offset, block_size):
    score_scale = 1.0 / math.sqrt(queries.shape[2])
    allowed = block_mask(seg_row, group_row, length, offset, block_size)
    scores = (
        jnp.einsum(
            "qhd,khd->hqk",
            queries[offset : offset + block_size],
            key_rows,
            preferred_element_type=jnp.float32,
        )
        * score_scale
    )
    return jnp.where(allowed[None], scores, -1e30)


def attend_forward(pieces):
    queries, key_rows, values, seg_row, group_row, length = pieces
    seq_len = queries.shape[0]
    block_size = min(512, seq_len)
    context_parts = []
    sum_parts = []
    for offset in range(0, seq_len, block_size):
        scores = block_scores(queries, key_rows, seg_row, group_row, length, offset, block_size)
        row_top = jnp.max(scores, axis=-1, keepdims=True)
        exponent = jnp.exp(scores - row_top)
        row_total = jnp.sum(exponent, axis=-1, keepdims=True)
        probability = (exponent / row_total).astype(jnp.bfloat16)
        context_parts.append(
            jnp.einsum("hqk,khd->qhd", probability, values, preferred_element_type=jnp.float32)
        )
        sum_parts.append(row_top[..., 0] + jnp.log(row_total[..., 0]))
    return (jnp.concatenate(context_parts, 0), jnp.concatenate(sum_parts, 1))


def attend_backward(pieces):
    queries, key_rows, values, seg_row, group_row, length, log_sums, grad_out = pieces
    seq_len = queries.shape[0]
    block_size = min(512, seq_len)
    score_scale = 1.0 / math.sqrt(queries.shape[2])
    grad_query = []
    grad_key = jnp.zeros(key_rows.shape, jnp.float32)
    grad_value = jnp.zeros(values.shape, jnp.float32)
    for offset in range(0, seq_len, block_size):
        scores = block_scores(queries, key_rows, seg_row, group_row, length, offset, block_size)
        probability = jnp.exp(scores - log_sums[:, offset : offset + block_size, None])
        grad_block = grad_out[offset : offset + block_size]
        grad_prob = jnp.einsum(
            "qhd,khd->hqk", grad_block, values, preferred_element_type=jnp.float32
        )
        inner = jnp.sum(probability * grad_prob, axis=-1, keepdims=True)
        grad_score = (probability * (grad_prob - inner)).astype(jnp.bfloat16)
        grad_query.append(
            jnp.einsum("hqk,khd->qhd", grad_score, key_rows, preferred_element_type=jnp.float32)
            * score_scale
        )
        grad_key = (
            grad_key
            + jnp.einsum(
                "hqk,qhd->khd",
                grad_score,
                queries[offset : offset + block_size],
                preferred_element_type=jnp.float32,
            )
            * score_scale
        )
        grad_value = grad_value + jnp.einsum(
            "hqk,qhd->khd",
            probability.astype(jnp.bfloat16),
            grad_block,
            preferred_element_type=jnp.float32,
        )
    return (jnp.concatenate(grad_query, 0), grad_key, grad_value)


def contract_rows(left_side, right_side):
    return lax.dot_general(
        left_side, right_side, (((0,), (0,)), ((), ())), preferred_element_type=jnp.float32
    )


def contract_cols(left_side, right_side):
    return lax.dot_general(
        left_side, right_side, (((1,), (1,)), ((), ())), preferred_element_type=jnp.float32
    )


def forward_use(signal, matrices, vector_rows, seg_rows, group_rows, lengths):
    row_count, seq_len = seg_rows.shape
    model_width = signal.shape[1]
    ff_width = vector_rows[8:].size
    low_signal = signal.astype(jnp.bfloat16)
    project_bias = jnp.concatenate([vector_rows[4], jnp.zeros_like(vector_rows[4]), vector_rows[5]])
    projected = (
        jnp.dot(low_signal, matrices[:, : 3 * model_width], preferred_element_type=jnp.float32)
        + project_bias
    ).astype(jnp.bfloat16)
    heads_view = projected.reshape(row_count, seq_len, 3, HEADS, model_width // HEADS)
    context, log_sums = lax.map(
        attend_forward,
        (
            heads_view[:, :, 0],
            heads_view[:, :, 1],
            heads_view[:, :, 2],
            seg_rows,
            group_rows,
            lengths,
        ),
    )
    context = context.reshape(row_count * seq_len, model_width).astype(jnp.bfloat16)
    attended = (
        jnp.dot(
            context,
            matrices[:, 3 * model_width : 4 * model_width],
            preferred_element_type=jnp.float32,
        )
        + vector_rows[6]
    )
    joined = signal + attended
    middle = layer_norm(joined, vector_rows[0], vector_rows[1])
    low_middle = middle.astype(jnp.bfloat16)
    hidden_pre = jnp.dot(
        low_middle,
        matrices[:, 4 * model_width : 4 * model_width + ff_width],
        preferred_element_type=jnp.float32,
    ) + vector_rows[8:].reshape(ff_width)
    activation = gelu_tanh(hidden_pre).astype(jnp.bfloat16)
    back_out = contract_cols(activation, matrices[:, 4 * model_width + ff_width :]) + vector_rows[7]
    summed = middle + back_out
    result = layer_norm(summed, vector_rows[2], vector_rows[3])
    stored = (
        low_signal,
        heads_view,
        context,
        log_sums,
        joined,
        low_middle,
        hidden_pre,
        activation,
        summed,
    )
    return (result, stored)


def backward_use(grad_result, stored, matrices, vector_rows, seg_rows, group_rows, lengths):
    (
        low_signal,
        heads_view,
        context,
        log_sums,
        joined,
        low_middle,
        hidden_pre,
        activation,
        summed,
    ) = stored
    row_count, seq_len = seg_rows.shape
    model_width = low_signal.shape[1]
    ff_width = hidden_pre.shape[1]
    normed_two, pull_two = jax.vjp(layer_norm, summed, vector_rows[2], vector_rows[3])
    grad_summed, grad_gain_two, grad_shift_two = pull_two(grad_result)
    grad_back = grad_summed.astype(jnp.bfloat16)
    bias_back = jnp.sum(grad_back.astype(jnp.float32), axis=0)
    weight_back = contract_rows(grad_back, activation)
    grad_act = jnp.dot(
        grad_back, matrices[:, 4 * model_width + ff_width :], preferred_element_type=jnp.float32
    )
    gelu_out, pull_gelu = jax.vjp(gelu_tanh, hidden_pre)
    grad_pre = pull_gelu(grad_act)[0].astype(jnp.bfloat16)
    bias_in = jnp.sum(grad_pre.astype(jnp.float32), axis=0)
    weight_in = contract_rows(low_middle, grad_pre)
    grad_middle = grad_summed + contract_cols(
        grad_pre, matrices[:, 4 * model_width : 4 * model_width + ff_width]
    )
    normed_one, pull_one = jax.vjp(layer_norm, joined, vector_rows[0], vector_rows[1])
    grad_joined, grad_gain_one, grad_shift_one = pull_one(grad_middle)
    grad_attn = grad_joined.astype(jnp.bfloat16)
    bias_out = jnp.sum(grad_attn.astype(jnp.float32), axis=0)
    weight_out = contract_rows(context, grad_attn)
    grad_context = contract_cols(grad_attn, matrices[:, 3 * model_width : 4 * model_width]).astype(
        jnp.bfloat16
    )
    grad_context = grad_context.reshape(row_count, seq_len, HEADS, model_width // HEADS)
    grad_query, grad_key, grad_value = lax.map(
        attend_backward,
        (
            heads_view[:, :, 0],
            heads_view[:, :, 1],
            heads_view[:, :, 2],
            seg_rows,
            group_rows,
            lengths,
            log_sums,
            grad_context,
        ),
    )
    grad_proj = (
        jnp.stack([grad_query, grad_key, grad_value], axis=2)
        .reshape(row_count * seq_len, 3 * model_width)
        .astype(jnp.bfloat16)
    )
    bias_sums = jnp.sum(grad_proj.astype(jnp.float32), axis=0)
    weight_qkv = contract_rows(low_signal, grad_proj)
    grad_signal = grad_joined + contract_cols(grad_proj, matrices[:, : 3 * model_width])
    weight_grad = jnp.concatenate([weight_qkv, weight_out, weight_in, weight_back], axis=1)
    small_rows = jnp.stack(
        [
            grad_gain_one,
            grad_shift_one,
            grad_gain_two,
            grad_shift_two,
            bias_sums[:model_width],
            bias_sums[2 * model_width :],
            bias_out,
            bias_back,
        ]
    )
    vector_grad = jnp.concatenate(
        [small_rows, bias_in.reshape(ff_width // model_width, model_width)], axis=0
    )
    return (grad_signal, weight_grad, vector_grad)


def on_device(
    inputs,
    cotangent,
    lengths,
    segment_ids,
    group_tags,
    weights,
    first_moments,
    second_moments,
    vectors,
    vector_first,
    vector_second,
):
    matrices, low_vectors = (
        lax.all_gather(weights.astype(jnp.bfloat16), "shard", axis=0, tiled=True),
        lax.all_gather(vectors.astype(jnp.bfloat16), "shard", axis=1, tiled=True),
    )
    vector_rows = low_vectors.astype(jnp.float32)
    row_count, seq_len, model_width = inputs.shape
    group_rows = group_of(segment_ids, group_tags)
    begin_acts = inputs.astype(jnp.float32).reshape(row_count * seq_len, model_width)
    first_out, first_stored = forward_use(
        begin_acts, matrices, vector_rows, segment_ids, group_rows, lengths
    )
    second_out, second_stored = forward_use(
        first_out, matrices, vector_rows, segment_ids, group_rows, lengths
    )
    grad_top = cotangent.astype(jnp.float32).reshape(row_count * seq_len, model_width)
    grad_middle, weight_two, vector_two = backward_use(
        grad_top, second_stored, matrices, vector_rows, segment_ids, group_rows, lengths
    )
    grad_input, weight_one, vector_one = backward_use(
        grad_middle, first_stored, matrices, vector_rows, segment_ids, group_rows, lengths
    )
    weight_grad = weight_one + weight_two
    vector_grad = vector_one + vector_two
    own_weight, own_vector = (
        lax.psum_scatter(
            weight_grad.astype(jnp.bfloat16), "shard", scatter_dimension=0, tiled=True
        ).astype(jnp.float32),
        lax.psum_scatter(
            vector_grad.astype(jnp.bfloat16), "shard", scatter_dimension=1, tiled=True
        ).astype(jnp.float32),
    )
    own_weight, own_vector = (
        lax.psum(own_weight.astype(jnp.bfloat16), "batch").astype(jnp.float32),
        lax.psum(own_vector.astype(jnp.bfloat16), "batch").astype(jnp.float32),
    )
    squares = lax.psum(jnp.sum(own_weight * own_weight) + jnp.sum(own_vector * own_vector), "shard")
    grad_norm = jnp.sqrt(squares)
    clip_limit = math.sqrt(D * WCOLS)
    factor = clip_limit / jnp.maximum(grad_norm, clip_limit)
    new_weights, new_first, new_second = adam_update(
        weights, first_moments, second_moments, own_weight * factor
    )
    new_vectors, new_vector_first, new_vector_second = adam_update(
        vectors, vector_first, vector_second, own_vector * factor
    )
    outputs = second_out.reshape(row_count, seq_len, model_width).astype(jnp.bfloat16)
    input_grad = grad_input.reshape(row_count, seq_len, model_width)
    return (
        outputs,
        input_grad,
        own_weight,
        own_vector,
        grad_norm,
        new_weights,
        new_first,
        new_second,
        new_vectors,
        new_vector_first,
        new_vector_second,
    )


def solution(mesh):
    placed = (
        P(("batch", "shard"), None, None),
        P(("batch", "shard"), None, None),
        P(("batch", "shard")),
        P(("batch", "shard"), None),
        P(("batch", "shard"), None),
        P("shard", None),
        P("shard", None),
        P("shard", None),
        P(None, "shard"),
        P(None, "shard"),
        P(None, "shard"),
    )
    return jax.shard_map(
        on_device,
        mesh=mesh,
        in_specs=placed,
        out_specs=(
            P(("batch", "shard"), None, None),
            P(("batch", "shard"), None, None),
            P("shard", None),
            P(None, "shard"),
            P(),
            P("shard", None),
            P("shard", None),
            P("shard", None),
            P(None, "shard"),
            P(None, "shard"),
            P(None, "shard"),
        ),
        check_vma=False,
    )
```

profile of v0, /device:TPU:0, one launch (start us, length us, event | category | flops | bytes accessed | tf_op | source)
XLA Modules:
  0.0 708.9 jit_solution(13713381901005244235)
XLA Ops:
  11.4 13.5 %all_gather.7 = bf16[12,512]{1,0:T(8,128)(2,1)S(1)} all-gather(bf16[12,128]{1,0:T(8,128)(2,1)S(1)} %convert_element_type.213), channel_id=1, replica_groups=mesh['batch'=8,'shard'=4] {'shard'}, dimensions={1}, use_global_device_ids=true | all-gather | bytes 15360 | tf_op jit(solution)/shard_map/all_gather | solution.py:305
  30.1 98.8 %all-gather.2.cloned.1.call-done = bf16[512,6144]{1,0:T(8,128)(2,1)} async-done(((bf16[128,6144]{1,0:T(8,128)(2,1)}), bf16[512,6144]{1,0:T(8,128)(2,1)}) %all-gather.2.cloned.1.call-update) | async-done | bytes 6291472 | tf_op jit(solution)/shard_map/all_gather | solution.py:304
  128.9 4.9 add_convert_fusion.1
  136.9 4.6 fusion.125
  160.1 4.0 fusion.77
  167.8 8.6 %multiply_convert_fusion.5 = (bf16[1024,2048]{1,0:T(8,128)(2,1)S(1)}, f32[1024,2048]{1,0:T(8,128)}) fusion(f32[2048]{0:T(1024)S(1)} %bitcast.298, bf16[512,6144]{1,0:T(8,128)(2,1)} %all-gather.2.cloned.1.call-done, f32[1024,512]{0,1:T(8,128)S(1)} %get-tuple-element.252, f32[512]{0:T(512)S(1)} %bitcast.305, f32[512]{0:T(512)S(1)} %bitcast.275, ...), kind=kOutput, calls=%fused_computation.65 | convolution fusion | flops 2171076608 | bytes 16797696 | tf_op jit(solution)/shard_map/dot_general | solution.py:188
  184.0 4.9 copy.72
  188.9 4.6 fusion.129
  197.9 4.2 fusion.80
  202.2 7.5 %fusion.130 = (f32[8,512]{1,0:T(8,128)S(1)}, f32[8,512,1024]{2,1,0:T(8,128)}) fusion(bf16[1,1024,3,8,64]{1,4,3,2,0:T(8,128)(2,1)S(1)} %bitcast.243, pred[512,1024]{1,0:T(8,128)(4,1)S(1)} %copy-done.19), kind=kOutput, calls=%fused_computation.249 | convolution fusion | flops 549449728 | bytes 18890752 | tf_op jit(solution)/shard_map/while/body/eval_jaxpr/qhd,khd->hqk/dot_general | solution.py:72
  209.6 7.7 %fusion.2 = f32[8,512]{1,0:T(8,128)S(1)} fusion(f32[8,512,1024]{2,1,0:T(8,128)} %get-tuple-element.260, f32[8,512]{1,0:T(8,128)S(1)} %get-tuple-element.259), kind=kLoop, calls=%fused_computation.26 | loop fusion | flops 8384512 | bytes 16809984 | tf_op jit(solution)/shard_map/while/body/eval_jaxpr/reduce_sum | solution.py:93
  217.9 7.6 %fusion.79 = bf16[512,8,64]{0,2,1:T(8,128)(2,1)S(1)} fusion(f32[8,512,1024]{2,1,0:T(8,128)} %get-tuple-element.260, f32[8,512]{1,0:T(8,128)S(1)} %fusion.2, f32[8,512]{1,0:T(8,128)S(1)} %get-tuple-element.259, bf16[1,1024,3,8,64]{1,4,3,2,0:T(8,128)(2,1)S(1)} %bitcast.244), kind=kOutput, calls=%fused_computation.165 | convolution fusion | flops 549715968 | bytes 18382848 | tf_op jit(solution)/shard_map/while/body/eval_jaxpr/hqk,khd->qhd/dot_general | solution.py:96
  228.2 9.7 %multiply_convert_fusion.4 = (bf16[1024,2048]{1,0:T(8,128)(2,1)}, f32[1024,2048]{1,0:T(8,128)}) fusion(f32[2048]{0:T(1024)S(1)} %bitcast.299, bf16[512,6144]{1,0:T(8,128)(2,1)} %all-gather.2.cloned.1.call-done, f32[1024,512]{0,1:T(8,128)S(1)} %get-tuple-element.262, f32[1024]{0:T(1024)S(1)} %fusion.101, f32[1024]{0:T(1024)S(1)} %broadcast_multiply_fusion.1, ...), kind=kOutput, calls=%fused_computation.64 | convolution fusion | flops 2171076608 | bytes 16797696 | tf_op jit(solution)/shard_map/dot_general | solution.py:188
  237.9 4.8 fusion.132
  247.5 4.3 fusion.136
  251.9 12.7 %convert_reduce_fusion = (f32[2048]{0:T(1024)}, bf16[1024,2048]{1,0:T(8,128)(2,1)}) fusion(bf16[1024,512]{0,1:T(8,128)(2,1)S(1)} %get-tuple-element.205, bf16[512,6144]{1,0:T(8,128)(2,1)S(1)} %bitcast.325, f32[1024,2048]{1,0:T(8,128)} %get-tuple-element.264, f32[2048]{0:T(1024)S(1)} %bitcast.300), kind=kOutput, calls=%fused_computation.58 | convolution fusion | flops 2204104704 | bytes 15745024 | tf_op jit(solution)/shard_map/dot_general | solution.py:231
  264.5 6.7 fusion.103
  271.2 6.3 multiply_reduce_fusion.5
  281.8 12.0 %multiply_reduce_fusion.3 = (f32[8,512]{1,0:T(8,128)}, f32[8,512,1024]{2,1,0:T(8,128)}) fusion(f32[8,512,1024]{2,1,0:T(8,128)} %get-tuple-element.260, f32[8,512]{1,0:T(8,128)} %log_add_fusion.3, bf16[512,8,64]{0,2,1:T(8,128)(2,1)S(1)} %bitcast.245, bf16[1,1024,3,8,64]{1,4,3,2,0:T(8,128)(2,1)} %bitcast.236), kind=kOutput, calls=%fused_computation.10 | convolution fusion | flops 549449728 | bytes 35160064 | tf_op jit(solution)/shard_map/while/body/eval_jaxpr/qhd,khd->hqk/dot_general | solution.py:114
  293.9 12.0 %multiply_convert_fusion.3 = bf16[8,512,1024]{2,1,0:T(8,128)(2,1)S(1)} fusion(f32[8,512,1024]{2,1,0:T(8,128)} %get-tuple-element.269, f32[8,512,1024]{2,1,0:T(8,128)} %get-tuple-element.260, f32[8,512]{1,0:T(8,128)} %get-tuple-element.268, f32[8,512]{1,0:T(8,128)} %log_add_fusion.3), kind=kLoop, calls=%fused_computation.9 | loop fusion | flops 16777216 | bytes 41975808 | tf_op jit(solution)/shard_map/while/body/eval_jaxpr/convert_element_type | solution.py:118
  305.9 4.7 fusion.56
  310.6 3.9 fusion.93
  314.5 3.9 fusion.25
  318.5 9.9 %multiply_reduce_fusion.2 = (f32[8,512]{1,0:T(8,128)}, f32[8,512,1024]{2,1,0:T(8,128)}) fusion(f32[8,512,1024]{2,1,0:T(8,128)S(1)} %get-tuple-element.258, f32[8,512]{1,0:T(8,128)} %log_add_fusion.2, bf16[512,8,64]{0,2,1:T(8,128)(2,1)S(1)} %bitcast.250, bf16[1,1024,3,8,64]{1,4,3,2,0:T(8,128)(2,1)} %bitcast.239), kind=kOutput, calls=%fused_computation.7 | convolution fusion | flops 549449728 | bytes 35160064 | tf_op jit(solution)/shard_map/while/body/eval_jaxpr/qhd,khd->hqk/dot_general | solution.py:114
  328.4 9.0 %add_bitcast_fusion.2 = bf16[1,1024,1,8,64]{1,4,3,2,0:T(8,128)(2,1)} fusion(f32[8,64,1024]{2,1,0:T(8,128)} %fusion.25, bf16[512,8,64]{0,2,1:T(8,128)(2,1)S(1)} %bitcast.246, f32[8,512,1024]{2,1,0:T(8,128)} %get-tuple-element.260, f32[8,512]{1,0:T(8,128)} %log_add_fusion.3), kind=kOutput, calls=%fused_computation.108 | convolution fusion | flops 546308096 | bytes 20463616 | tf_op jit(solution)/shard_map/while/body/eval_jaxpr/hqk,qhd->khd/dot_general | solution.py:133
  337.4 7.7 %multiply_convert_fusion.2 = bf16[8,512,1024]{2,1,0:T(8,128)(2,1)S(1)} fusion(f32[8,512,1024]{2,1,0:T(8,128)} %get-tuple-element.271, f32[8,512,1024]{2,1,0:T(8,128)S(1)} %get-tuple-element.258, f32[8,512]{1,0:T(8,128)S(1)} %copy-done.36, f32[8,512]{1,0:T(8,128)S(1)} %copy-done.35), kind=kLoop, calls=%fused_computation.6 | loop fusion | flops 16777216 | bytes 41975808 | tf_op jit(solution)/shard_map/while/body/eval_jaxpr/convert_element_type | solution.py:118
  345.1 4.0 fusion.55
  362.7 4.4 fusion.134
  367.1 9.9 %convert_reduce_fusion.1 = (f32[2048]{0:T(1024)}, bf16[1024,2048]{1,0:T(8,128)(2,1)S(1)}) fusion(bf16[1024,512]{0,1:T(8,128)(2,1)S(1)} %get-tuple-element.211, bf16[512,6144]{1,0:T(8,128)(2,1)S(1)} %bitcast.327, f32[1024,2048]{1,0:T(8,128)S(1)} %bitcast.329, f32[2048]{0:T(1024)S(1)} %bitcast.301), kind=kOutput, calls=%fused_computation.59 | convolution fusion | flops 2204104704 | bytes 15745024 | tf_op jit(solution)/shard_map/dot_general | solution.py:231
  377.1 4.4 fusion.109
  390.6 9.9 %multiply_reduce_fusion.1 = (f32[8,512]{1,0:T(8,128)}, f32[8,512,1024]{2,1,0:T(8,128)}) fusion(f32[8,512,1024]{2,1,0:T(8,128)S(1)} %bitcast.224, f32[8,512]{1,0:T(8,128)} %log_add_fusion.1, bf16[512,8,64]{0,2,1:T(8,128)(2,1)S(1)} %bitcast.247, bf16[1,1024,3,8,64]{1,4,3,2,0:T(8,128)(2,1)} %bitcast.229), kind=kOutput, calls=%fused_computation.4 | convolution fusion | flops 549449728 | bytes 35160064 | tf_op jit(solution)/shard_map/while/body/eval_jaxpr/qhd,khd->hqk/dot_general | solution.py:114
  400.5 12.4 %multiply_convert_fusion.1 = bf16[8,512,1024]{2,1,0:T(8,128)(2,1)S(1)} fusion(f32[8,512,1024]{2,1,0:T(8,128)} %get-tuple-element.275, f32[8,512,1024]{2,1,0:T(8,128)} %copy-done.1, f32[8,512]{1,0:T(8,128)} %get-tuple-element.274, f32[8,512]{1,0:T(8,128)} %log_add_fusion.1), kind=kLoop, calls=%fused_computation.3 | loop fusion | flops 16777216 | bytes 41975808 | tf_op jit(solution)/shard_map/while/body/eval_jaxpr/convert_element_type | solution.py:118
  412.9 5.6 fusion.54
  418.5 3.9 fusion.92
  422.5 4.0 fusion.21
  426.4 9.8 %multiply_reduce_fusion = (f32[8,512]{1,0:T(8,128)}, f32[8,512,1024]{2,1,0:T(8,128)}) fusion(f32[8,512,1024]{2,1,0:T(8,128)S(1)} %bitcast.222, f32[8,512]{1,0:T(8,128)} %log_add_fusion, bf16[512,8,64]{0,2,1:T(8,128)(2,1)S(1)} %bitcast.252, bf16[1,1024,3,8,64]{1,4,3,2,0:T(8,128)(2,1)} %bitcast.232), kind=kOutput, calls=%fused_computation.1 | convolution fusion | flops 549449728 | bytes 35160064 | tf_op jit(solution)/shard_map/while/body/eval_jaxpr/qhd,khd->hqk/dot_general | solution.py:114
  436.3 9.0 %add_bitcast_fusion.1 = bf16[1,1024,1,8,64]{1,4,3,2,0:T(8,128)(2,1)} fusion(f32[8,64,1024]{2,1,0:T(8,128)} %fusion.21, bf16[512,8,64]{0,2,1:T(8,128)(2,1)S(1)} %bitcast.248, f32[8,512,1024]{2,1,0:T(8,128)} %copy-done.1, f32[8,512]{1,0:T(8,128)} %log_add_fusion.1), kind=kOutput, calls=%fused_computation.104 | convolution fusion | flops 546308096 | bytes 20463616 | tf_op jit(solution)/shard_map/while/body/eval_jaxpr/hqk,qhd->khd/dot_general | solution.py:133
  445.3 7.7 %multiply_convert_fusion = bf16[8,512,1024]{2,1,0:T(8,128)(2,1)S(1)} fusion(f32[8,512,1024]{2,1,0:T(8,128)} %get-tuple-element.277, f32[8,512,1024]{2,1,0:T(8,128)S(1)} %bitcast.222, f32[8,512]{1,0:T(8,128)S(1)} %copy-done.37, f32[8,512]{1,0:T(8,128)S(1)} %copy-done.33), kind=kLoop, calls=%fused_computation | loop fusion | flops 16777216 | bytes 41975808 | tf_op jit(solution)/shard_map/while/body/eval_jaxpr/convert_element_type | solution.py:118
  453.0 4.0 fusion.53
  468.4 10.4 %fusion.8 = bf16[512,6144]{1,0:T(8,128)(2,1)} fusion(f32[512,2048]{1,0:T(8,128)} %fusion.134, f32[512,2048]{1,0:T(8,128)} %fusion.109, f32[512,512]{1,0:T(8,128)} %fusion.133, f32[512,1536]{1,0:T(8,128)S(1)} %copy.79, f32[512,2048]{1,0:T(8,128)} %fusion.136, f32[512,2048]{1,0:T(8,128)} %fusion.103, f32[512,512]{1,0:T(8,128)} %fusion.135, f32[512,1536]{1,0:T(8,128)} %fusion.106), kind=kLoop, calls=%fused_computation.33 | loop fusion | flops 25165824 | bytes 31457280 | tf_op jit(solution)/shard_map/convert_element_type | solution.py:328
  483.9 104.2 %reduce-scatter.5.cloned.1.call-done = bf16[128,6144]{1,0:T(8,128)(2,1)} async-done(((bf16[512,6144]{1,0:T(8,128)(2,1)}), bf16[128,6144]{1,0:T(8,128)(2,1)}) %reduce-scatter.5.cloned.1.call-update) | async-done | bytes 1572880 | tf_op jit(solution)/shard_map/reduce_scatter | solution.py:327
  588.1 5.5 add_bitcast_fusion
  593.6 17.1 %reduce-scatter.7.cloned.1.call-done = bf16[128,12]{1,0:T(8,128)(2,1)} async-done(((bf16[512,12]{1,0:T(8,128)(2,1)}), bf16[128,12]{1,0:T(8,128)(2,1)}) %reduce-scatter.7.cloned.1.call-update) | async-done | bytes 3088
  611.5 12.0 %psum.22 = bf16[12,128]{1,0:T(8,128)(2,1)S(1)} all-reduce(bf16[12,128]{1,0:T(8,128)(2,1)S(1)} %copy.92), channel_id=1, replica_groups=mesh['batch'=8,'shard'=4] {'batch'}, use_global_device_ids=true, to_apply=%region_48.49 | all-reduce | flops 1536 | bytes 6144 | tf_op jit(solution)/shard_map/psum | solution.py:336
  624.1 47.1 %all-reduce.2.cloned.1.call-done = bf16[128,6144]{1,0:T(8,128)(2,1)} async-done(((bf16[128,6144]{1,0:T(8,128)(2,1)}), bf16[128,6144]{1,0:T(8,128)(2,1)}) %all-reduce.2.cloned.1.call-update) | async-done | bytes 1572880 | tf_op jit(solution)/shard_map/psum | solution.py:335
  671.2 4.4 multiply_reduce_fusion.4
  680.2 12.3 %psum.23 = f32[]{:T(128)} all-reduce(f32[]{:T(128)S(6)} %add.359), channel_id=1, replica_groups=mesh['batch'=8,'shard'=4] {'shard'}, use_global_device_ids=true, to_apply=%region_51.52 | all-reduce | flops 1 | bytes 8 | tf_op jit(solution)/shard_map/psum | solution.py:338
  693.9 6.9 multiply_subtract_fusion
  (296 shorter events, 101.7 us)
Async XLA Ops:
  7.2 17.7 %copy-start.26 = (bf16[1,1024,512]{2,1,0:T(8,128)(2,1)S(1)}, bf16[1,1024,512]{2,1,0:T(8,128)(2,1)}, u32[]{:S(2)}) copy-start(bf16[1,1024,512]{2,1,0:T(8,128)(2,1)} %param.12) | copy-start | bytes 3145732
  7.2 19.1 %copy-start.27 = (bf16[1,1024,512]{2,1,0:T(8,128)(2,1)S(1)}, bf16[1,1024,512]{2,1,0:T(8,128)(2,1)}, u32[]{:S(2)}) copy-start(bf16[1,1024,512]{2,1,0:T(8,128)(2,1)} %param.11) | copy-start | bytes 3145732
  7.2 121.6 %all-gather.2.cloned.1.call-start = ((), (), s32[]{:S(2)}) async-start(), calls=%async_computation.2 | async-start | bytes 7864320 | tf_op jit(solution)/shard_map/all_gather | solution.py:304
  10.6 17.0 %copy-start.42 = (s32[1,1024]{1,0:T(1,128)S(1)}, s32[1,1024]{1,0:T(1,128)}, u32[]{:S(2)}) copy-start(s32[1,1024]{1,0:T(1,128)} %param.14) | copy-start | bytes 12292
  10.6 17.0 %copy-start.74 = (s32[1,8]{1,0:T(1,128)S(1)}, s32[1,8]{1,0:T(1,128)}, u32[]{:S(2)}) copy-start(s32[1,8]{1,0:T(1,128)} %param.15) | copy-start | bytes 100
  10.6 577.5 %reduce-scatter.5.cloned.1.call-start = ((), (), s32[]{:S(2)}) async-start(), calls=%async_computation.3 | async-start | bytes 7864320 | tf_op jit(solution)/shard_map/reduce_scatter | solution.py:327
  24.9 226.9 %copy-start.61 = (f32[1,4,4,128]{3,1,2,0:T(4,128)}, f32[1,4,4,128]{3,1,2,0:T(4,128)S(1)}, u32[]{:S(2)}) copy-start(f32[1,4,4,128]{3,1,2,0:T(4,128)S(1)} %copy.93) | copy-start | bytes 24580
  27.6 217.4 %copy-start.57 = (f32[1,512]{1,0:T(1,128)}, f32[1,512]{1,0:T(1,128)S(1)}, u32[]{:S(2)}) copy-start(f32[1,512]{1,0:T(1,128)S(1)} %get-tuple-element.228) | copy-start | bytes 6148
  27.6 236.9 %copy-start.66 = (f32[1,512]{1,0:T(1,128)}, f32[1,512]{1,0:T(1,128)S(1)}, u32[]{:S(2)}) copy-start(f32[1,512]{1,0:T(1,128)S(1)} %get-tuple-element.231) | copy-start | bytes 6148
  136.9 22.4 %copy-start.2 = (bf16[1024,1536]{0,1:T(8,128)(2,1)}, bf16[1024,1536]{0,1:T(8,128)(2,1)S(1)}, u32[]{:S(2)}) copy-start(bf16[1024,1536]{0,1:T(8,128)(2,1)S(1)} %copy.71) | copy-start | bytes 9437188
  141.6 5.8 copy-start
  154.4 5.7 copy-start.1
  164.2 12.2 %slice-start.8 = ((s8[6291456]{0:T(1024)(128)(4,1)}), s8[4194304]{0:T(1024)(128)(4,1)S(1)}, s32[]{:S(2)}) async-start(s8[6291456]{0:T(1024)(128)(4,1)} %bitcast.322), calls=%async_computation.14 | async-start | bytes 8388608
  166.5 9.9 %copy-start.9 = (f32[1024,512]{0,1:T(8,128)}, f32[1024,512]{0,1:T(8,128)S(1)}, u32[]{:S(2)}) copy-start(f32[1024,512]{0,1:T(8,128)S(1)} %get-tuple-element.252) | copy-start | bytes 6291460
  166.5 9.8 %copy-start.43 = (f32[1024]{0:T(1024)}, f32[1024]{0:T(1024)S(1)}, u32[]{:S(2)}) copy-start(f32[1024]{0:T(1024)S(1)} %broadcast_multiply_fusion.3) | copy-start | bytes 12292
  167.8 8.6 %copy-start.51 = (f32[1024]{0:T(1024)}, f32[1024]{0:T(1024)S(1)}, u32[]{:S(2)}) copy-start(f32[1024]{0:T(1024)S(1)} %fusion.99) | copy-start | bytes 12292
  167.8 8.6 %slice-start.9 = ((s8[6291456]{0:T(1024)(128)(4,1)}), s8[2097152]{0:T(1024)(128)(4,1)S(1)}, s32[]{:S(2)}) async-start(s8[6291456]{0:T(1024)(128)(4,1)} %bitcast.322), calls=%async_computation.15 | async-start | bytes 4194304
  180.3 45.4 %copy-start.53 = (f32[1024]{0:T(1024)}, f32[1024]{0:T(1024)S(1)}, u32[]{:S(2)}) copy-start(f32[1024]{0:T(1024)S(1)} %fusion.100) | copy-start | bytes 12292
  184.0 4.9 copy-start.20
  217.9 7.8 %copy-start.12 = (f32[1024,512]{0,1:T(8,128)S(1)}, f32[1024,512]{0,1:T(8,128)}, u32[]{:S(2)}) copy-start(f32[1024,512]{0,1:T(8,128)} %copy-done.11) | copy-start | bytes 6291460
  225.7 12.2 %slice-start.10 = ((s8[6291456]{0:T(1024)(128)(4,1)}), s8[4194304]{0:T(1024)(128)(4,1)S(1)}, s32[]{:S(2)}) async-start(s8[6291456]{0:T(1024)(128)(4,1)} %bitcast.324), calls=%async_computation.16 | async-start | bytes 8388608
  228.2 9.7 %slice-start.11 = ((s8[6291456]{0:T(1024)(128)(4,1)}), s8[2097152]{0:T(1024)(128)(4,1)S(1)}, s32[]{:S(2)}) async-start(s8[6291456]{0:T(1024)(128)(4,1)} %bitcast.324), calls=%async_computation.17 | async-start | bytes 4194304
  237.9 4.8 copy-start.4
  328.4 9.0 %copy-start.35 = (f32[8,512]{1,0:T(8,128)S(1)}, f32[8,512]{1,0:T(8,128)}, u32[]{:S(2)}) copy-start(f32[8,512]{1,0:T(8,128)} %log_add_fusion.2) | copy-start | bytes 49156
  328.4 9.0 %copy-start.36 = (f32[8,512]{1,0:T(8,128)S(1)}, f32[8,512]{1,0:T(8,128)}, u32[]{:S(2)}) copy-start(f32[8,512]{1,0:T(8,128)} %get-tuple-element.270) | copy-start | bytes 49156
  352.1 5.3 slice-start.12
  360.5 6.6 slice-start.14
  367.1 10.0 %copy-start.10 = (f32[1024,512]{0,1:T(8,128)S(1)}, f32[1024,512]{0,1:T(8,128)}, u32[]{:S(2)}) copy-start(f32[1024,512]{0,1:T(8,128)} %copy-done.9) | copy-start | bytes 6291460
  367.1 10.0 %copy-start.44 = (f32[1024]{0:T(1024)S(1)}, f32[1024]{0:T(1024)}, u32[]{:S(2)}) copy-start(f32[1024]{0:T(1024)} %copy-done.43) | copy-start | bytes 12292
  367.1 10.0 %copy-start.52 = (f32[1024]{0:T(1024)S(1)}, f32[1024]{0:T(1024)}, u32[]{:S(2)}) copy-start(f32[1024]{0:T(1024)} %copy-done.51) | copy-start | bytes 12292
  367.1 9.9 %copy-start.67 = (f32[1,512]{1,0:T(1,128)S(1)}, f32[1,512]{1,0:T(1,128)}, u32[]{:S(2)}) copy-start(f32[1,512]{1,0:T(1,128)} %copy-done.66) | copy-start | bytes 6148
  381.5 9.0 %slice-start.4 = ((s8[16777216]{0:T(1024)(128)(4,1)}), s8[4194304]{0:T(1024)(128)(4,1)S(1)}, s32[]{:S(2)}) async-start(s8[16777216]{0:T(1024)(128)(4,1)} %bitcast.223), calls=%async_computation.10 | async-start | bytes 8388608
  381.5 9.0 %slice-start.5 = ((s8[16777216]{0:T(1024)(128)(4,1)}), s8[4194304]{0:T(1024)(128)(4,1)S(1)}, s32[]{:S(2)}) async-start(s8[16777216]{0:T(1024)(128)(4,1)} %bitcast.223), calls=%async_computation.11 | async-start | bytes 8388608
  385.2 5.4 slice-start.6
  400.5 22.0 %slice-start = ((s8[16777216]{0:T(1024)(128)(4,1)}), s8[4194304]{0:T(1024)(128)(4,1)S(1)}, s32[]{:S(2)}) async-start(s8[16777216]{0:T(1024)(128)(4,1)} %bitcast.221), calls=%async_computation.6 | async-start | bytes 8388608
  400.5 22.0 %slice-start.1 = ((s8[16777216]{0:T(1024)(128)(4,1)}), s8[4194304]{0:T(1024)(128)(4,1)S(1)}, s32[]{:S(2)}) async-start(s8[16777216]{0:T(1024)(128)(4,1)} %bitcast.221), calls=%async_computation.7 | async-start | bytes 8388608
  400.5 22.0 %slice-start.2 = ((s8[16777216]{0:T(1024)(128)(4,1)}), s8[4194304]{0:T(1024)(128)(4,1)S(1)}, s32[]{:S(2)}) async-start(s8[16777216]{0:T(1024)(128)(4,1)} %bitcast.221), calls=%async_computation.8 | async-start | bytes 8388608
  412.9 9.5 %slice-start.3 = ((s8[16777216]{0:T(1024)(128)(4,1)}), s8[4194304]{0:T(1024)(128)(4,1)S(1)}, s32[]{:S(2)}) async-start(s8[16777216]{0:T(1024)(128)(4,1)} %bitcast.221), calls=%async_computation.9 | async-start | bytes 8388608
  436.3 9.1 %copy-start.33 = (f32[8,512]{1,0:T(8,128)S(1)}, f32[8,512]{1,0:T(8,128)}, u32[]{:S(2)}) copy-start(f32[8,512]{1,0:T(8,128)} %log_add_fusion) | copy-start | bytes 49156
  436.3 9.1 %copy-start.37 = (f32[8,512]{1,0:T(8,128)S(1)}, f32[8,512]{1,0:T(8,128)}, u32[]{:S(2)}) copy-start(f32[8,512]{1,0:T(8,128)} %get-tuple-element.276) | copy-start | bytes 49156
  479.0 109.2 %copy-start.15 = (f32[1024,512]{0,1:T(8,128)S(1)}, f32[1024,512]{0,1:T(8,128)}, u32[]{:S(2)}) copy-start(f32[1024,512]{0,1:T(8,128)} %copy-done.14) | copy-start | bytes 6291460
  479.0 131.7 %reduce-scatter.7.cloned.1.call-start = ((), (), s32[]{:S(2)}) async-start(), calls=%async_computation.5 | async-start | bytes 163840
  481.6 189.6 %all-reduce.2.cloned.1.call-start = ((), (), s32[]{:S(2)}) async-start(), calls=%async_computation.4 | async-start | bytes 3145728 | tf_op jit(solution)/shard_map/psum | solution.py:335
  624.1 69.1 %copy-start.48 = (f32[12,128]{1,0:T(8,128)}, f32[12,128]{1,0:T(8,128)S(1)}, u32[]{:S(2)}) copy-start(f32[12,128]{1,0:T(8,128)S(1)} %get-tuple-element.201) | copy-start | bytes 18436
  675.6 17.6 %copy-start.47 = (f32[12,128]{1,0:T(8,128)S(1)}, f32[12,128]{1,0:T(8,128)}, u32[]{:S(2)}) copy-start(f32[12,128]{1,0:T(8,128)} %param.19) | copy-start | bytes 18436
  675.6 17.6 %copy-start.59 = (f32[12,128]{1,0:T(8,128)S(1)}, f32[12,128]{1,0:T(8,128)}, u32[]{:S(2)}) copy-start(f32[12,128]{1,0:T(8,128)} %param.20) | copy-start | bytes 18436
  675.6 17.6 %copy-start.60 = (f32[12,128]{1,0:T(8,128)S(1)}, f32[12,128]{1,0:T(8,128)}, u32[]{:S(2)}) copy-start(f32[12,128]{1,0:T(8,128)} %param.21) | copy-start | bytes 18436
  675.7 18.3 %copy-start.8 = (f32[128,6144]{1,0:T(8,128)S(1)}, f32[128,6144]{1,0:T(8,128)}, u32[]{:S(2)}) copy-start(f32[128,6144]{1,0:T(8,128)} %param.16) | copy-start | bytes 9437188
  (50 other events, 135.8 us)
Sparse Core Ops, SparseCore 0:
  10.8 118.0 all-gather.1
  479.1 108.9 reduce-scatter.4
  590.9 19.7 reduce-scatter.6
  614.1 57.0 all-reduce.1
where the time goes:
time: 719 us; the launch traced here: 709 us
  waiting for transfers between devices  267 us (37%)
  matrix products  250 us (35%)
  other arithmetic  104 us (14%)
  blocking collectives  37.9 us (5%)
  local copies, waits for them, and re-layouts  30.2 us (4%)
  between operations  19.7 us (3%)
    reduce_scatter x1, waiting for transfers between devices, on_device(): lax.psum_scatter(weight_grad.astype(jnp.bfloat16), 'shard', scatter_dimen...  104 us
    all_gather x1, waiting for transfers between devices, on_device(): lax.all_gather(weights.astype(jnp.bfloat16), 'shard', axis=0, tiled=True)  98.8 us
    psum x1, waiting for transfers between devices, on_device(): lax.psum(own_weight.astype(jnp.bfloat16), 'batch').astype(jnp.float32)  47.1 us
    dot_general x4, matrix products, attend_backward(): jnp.einsum('qhd,khd->hqk', grad_block, values, preferred_element_type=jnp...  41.6 us
    convert_element_type x4, other arithmetic, attend_backward(): grad_score = (probability * (grad_prob - inner)).astype(jnp.bfloat16)  39.8 us
    dot_general x8, matrix products, contract_rows(): lax.dot_general(left_side, right_side, (((0,), (0,)), ((), ())), preferre...  30.4 us
    dot_general x8, matrix products, contract_cols(): lax.dot_general(left_side, right_side, (((1,), (1,)), ((), ())), preferre...  27.2 us
    dot_general x4, matrix products, attend_backward(): jnp.einsum('hqk,qhd->khd', probability.astype(jnp.bfloat16), grad_block,...  26 us
  transfers between devices with their start and end apart: 4, of which 4 were waited for; matrix products, arithmetic and copies ran while one was open for 2% of the time, Pallas kernels for 0%

commit v1 on v0

v1 whole, which is shorter than its diff:
```python
import functools
import math

import jax
import jax.numpy as jnp
from jax import lax
from jax.experimental import pallas as pl
from jax.experimental.pallas import tpu as pltpu
from jax.sharding import PartitionSpec as P

D = 512
FF = 2048
HEADS = 8
HEAD_DIM = 64
STEP = 10
WCOLS = 6144

NORM_EPS = 1e-05
BETA_ONE = 0.5
BETA_TWO = 0.5
ADAM_EPS = 1e-08
DECAY = 0.01
WARMUP = 4000.0
RATE_SCALE = 150000.0

BF = jnp.bfloat16
F32 = jnp.float32
FAR = 1e30
SAFE_SCORE = 60.0
TILE = 256
VMEM_BYTES = 60 << 20


def params():
    return pltpu.CompilerParams(vmem_limit_bytes=VMEM_BYTES)


def cost(flops, bytes_accessed, transcendentals=0):
    return pl.CostEstimate(flops=int(flops), bytes_accessed=int(bytes_accessed), transcendentals=int(transcendentals))


def dg(left, right, left_dim, right_dim):
    return lax.dot_general(
        left, right, (((left_dim,), (right_dim,)), ((), ())), preferred_element_type=F32
    )


def whole(shape):
    return pl.BlockSpec(shape, lambda i: (0,) * len(shape))


def adam_update(master, moment_one, moment_two, gradient):
    moment_one = BETA_ONE * moment_one + (1.0 - BETA_ONE) * gradient
    moment_two = BETA_TWO * moment_two + (1.0 - BETA_TWO) * gradient * gradient
    step_rate = RATE_SCALE * D ** (-0.5) * min(STEP ** (-0.5), STEP * WARMUP ** (-1.5))
    fixed_first = moment_one / (1.0 - BETA_ONE**STEP)
    fixed_second = moment_two / (1.0 - BETA_TWO**STEP)
    master = master - step_rate * (
        fixed_first / (jnp.sqrt(fixed_second) + ADAM_EPS) + DECAY * master
    )
    return (master, moment_one, moment_two)


def attend_kernel(act_ref, wq_ref, wk_ref, wv_ref, bq_ref, bv_ref, kmask_ref, qmask_ref, e_ref, ctx_ref, qkv_ref, stat_ref):
    act = act_ref[...]
    tokens = act.shape[1]
    q = (dg(wq_ref[...], act, 0, 0) + bq_ref[...]).astype(BF) * jnp.asarray(HEAD_DIM**-0.5, BF)
    k = dg(wk_ref[...], act, 0, 0).astype(BF)
    v = (dg(wv_ref[...], act, 0, 0) + bv_ref[...]).astype(BF)
    qkv_ref[0] = q
    qkv_ref[1] = k
    qkv_ref[2] = v
    dead = kmask_ref[4:5, :].astype(F32)
    bound = jnp.zeros((1, 1), F32)
    selves = []
    for h in range(2):
        rows = slice(h * HEAD_DIM, (h + 1) * HEAD_DIM)
        qf, kf = q[rows].astype(F32), k[rows].astype(F32)
        selves.append(jnp.sum(qf * kf, axis=0, keepdims=True))
        q_top = jnp.max(jnp.sum(qf * qf, axis=0, keepdims=True), axis=1, keepdims=True)
        k_top = jnp.max(jnp.sum(kf * kf, axis=0, keepdims=True), axis=1, keepdims=True)
        bound = jnp.maximum(bound, q_top * k_top)
    safe = bound[0, 0] <= SAFE_SCORE * SAFE_SCORE

    def scores(h):
        rows = slice(h * HEAD_DIM, (h + 1) * HEAD_DIM)
        keys = jnp.concatenate([k[rows], kmask_ref[...]], axis=0).T
        queries = jnp.concatenate([q[rows], qmask_ref[...]], axis=0)
        return dg(keys, queries, 1, 0)

    def finish(h, e, e_self):
        rows = slice(h * HEAD_DIM, (h + 1) * HEAD_DIM)
        low_e = e.astype(BF)
        e_ref[h] = low_e
        total = jnp.sum(e, axis=0, keepdims=True) + e_self
        scale = 1.0 / total
        values = v[rows]
        mixed = dg(values, low_e, 1, 0) + values.astype(F32) * e_self.astype(BF).astype(F32)
        ctx_ref[rows, :] = (mixed * scale).astype(BF)
        stat_ref[h, 0:1, :] = scale
        stat_ref[h, 1:2, :] = e_self

    @pl.when(safe)
    def _():
        for h in range(2):
            finish(h, jnp.exp(scores(h)), jnp.exp(selves[h]) * dead)

    @pl.when(jnp.logical_not(safe))
    def _():
        for h in range(2):
            s = scores(h)
            own = jnp.where(dead > 0, selves[h], -FAR)
            top = jnp.maximum(jnp.max(s, axis=0, keepdims=True), own)
            finish(h, jnp.exp(s - top), jnp.exp(own - top) * dead)


def attend(act, w_qkv, bias_q, bias_v, kmask, qmask):
    width, tokens = act.shape
    pairs = width // (2 * HEAD_DIM)
    pair = 2 * HEAD_DIM
    heads = width // HEAD_DIM
    return pl.pallas_call(
        attend_kernel,
        name="attend",
        grid=(pairs,),
        in_specs=[
            whole((width, tokens)),
            pl.BlockSpec((width, pair), lambda i: (0, i)),
            pl.BlockSpec((width, pair), lambda i: (0, pairs + i)),
            pl.BlockSpec((width, pair), lambda i: (0, 2 * pairs + i)),
            pl.BlockSpec((pair, 1), lambda i: (i, 0)),
            pl.BlockSpec((pair, 1), lambda i: (i, 0)),
            whole((16, tokens)),
            whole((16, tokens)),
        ],
        out_specs=[
            pl.BlockSpec((2, tokens, tokens), lambda i: (i, 0, 0)),
            pl.BlockSpec((pair, tokens), lambda i: (i, 0)),
            pl.BlockSpec((3, pair, tokens), lambda i: (0, i, 0)),
            pl.BlockSpec((2, 2, tokens), lambda i: (i, 0, 0)),
        ],
        out_shape=[
            jax.ShapeDtypeStruct((heads, tokens, tokens), BF),
            jax.ShapeDtypeStruct((width, tokens), BF),
            jax.ShapeDtypeStruct((3, width, tokens), BF),
            jax.ShapeDtypeStruct((heads, 2, tokens), F32),
        ],
        compiler_params=params(),
        cost_estimate=cost(6 * width * width * tokens + 4 * width * tokens * tokens, 2 * heads * tokens * tokens, heads * tokens * tokens),
    )(act, w_qkv, w_qkv, w_qkv, bias_q, bias_v, kmask, qmask)


def attend_back_kernel(e_ref, qkv_ref, stat_ref, grad_ref, inner_ref, out_ref, ds_ref):
    for h in range(2):
        rows = slice(h * HEAD_DIM, (h + 1) * HEAD_DIM)
        q, k, v = qkv_ref[0, rows], qkv_ref[1, rows], qkv_ref[2, rows]
        grad = grad_ref[rows]
        inner = inner_ref[h]
        e_self = stat_ref[h, 1:2, :]
        grad_f = grad.astype(F32)
        ds = (e_ref[h].astype(F32) * (dg(v.T, grad, 1, 0) - inner)).astype(BF)
        ds_ref[h] = ds
        own = (e_self * (jnp.sum(grad_f * v.astype(F32), axis=0, keepdims=True) - inner)).astype(BF).astype(F32)
        scale = HEAD_DIM**-0.5
        out_ref[0, rows] = ((dg(k, ds, 1, 0) + k.astype(F32) * own) * scale).astype(BF)
        out_ref[2, rows] = (dg(grad, e_ref[h], 1, 1) + grad_f * e_self.astype(BF).astype(F32)).astype(BF)
        out_ref[1, rows] = (dg(q, ds_ref[h], 1, 1) + q.astype(F32) * own).astype(BF)


def attend_back(e, qkv, stat, grad, inner):
    heads, tokens, _ = e.shape
    width = grad.shape[0]
    pairs = heads // 2
    pair = 2 * HEAD_DIM
    return pl.pallas_call(
        attend_back_kernel,
        name="attend_back",
        grid=(pairs,),
        in_specs=[
            pl.BlockSpec((2, tokens, tokens), lambda i: (i, 0, 0)),
            pl.BlockSpec((3, pair, tokens), lambda i: (0, i, 0)),
            pl.BlockSpec((2, 2, tokens), lambda i: (i, 0, 0)),
            pl.BlockSpec((pair, tokens), lambda i: (i, 0)),
            pl.BlockSpec((2, 1, tokens), lambda i: (i, 0, 0)),
        ],
        out_specs=pl.BlockSpec((3, pair, tokens), lambda i: (0, i, 0)),
        out_shape=jax.ShapeDtypeStruct((3, width, tokens), BF),
        scratch_shapes=[pltpu.VMEM((2, tokens, tokens), BF)],
        compiler_params=params(),
        cost_estimate=cost(8 * width * tokens * tokens, 2 * heads * tokens * tokens),
    )(e, qkv, stat, grad, inner)


def normed(t):
    mean = jnp.mean(t, axis=0, keepdims=True)
    centred = t - mean
    rstd = lax.rsqrt(jnp.mean(centred * centred, axis=0, keepdims=True) + NORM_EPS)
    return centred * rstd, rstd


def normed_back(grad, unit, rstd, gain):
    scaled = grad * gain
    mean = jnp.mean(scaled, axis=0, keepdims=True)
    along = jnp.mean(scaled * unit, axis=0, keepdims=True)
    return rstd * (scaled - mean - unit * along)


def gelu_and_slope(t):
    square = t * t
    inside = jnp.tanh(t * (0.7978845608028654 + (0.7978845608028654 * 0.044715) * square))
    half = 0.5 + 0.5 * inside
    slope = half + (t * (0.5 - 0.5 * inside * inside)) * (
        0.7978845608028654 + (3.0 * 0.7978845608028654 * 0.044715) * square
    )
    return t * half, slope


def lanes_sum(t):
    out = t[:, 0:128]
    for j in range(128, t.shape[1], 128):
        out = out + t[:, j : j + 128]
    return out


def dense_forward(signal, ctx, wo_ref, win_ref, wback_ref, col_ref, bin_ref):
    joined = signal + dg(wo_ref[...], ctx, 0, 0) + col_ref[:, 6:7]
    unit_one, rstd_one = normed(joined)
    middle = unit_one * col_ref[:, 0:1] + col_ref[:, 1:2]
    low_middle = middle.astype(BF)
    pre = dg(win_ref[...], low_middle, 0, 0) + bin_ref[...]
    gelu, slope = gelu_and_slope(pre)
    act = gelu.astype(BF)
    summed = middle + dg(wback_ref[...], act, 1, 0) + col_ref[:, 7:8]
    unit_two, rstd_two = normed(summed)
    return unit_one, rstd_one, low_middle, slope, act, unit_two, rstd_two


def dense_back(grad, unit_one, rstd_one, slope, unit_two, rstd_two, ctx, stat_ref, wo_ref, win_ref, wback_ref, col_ref,
               sums_ref, joined_ref, gctx_ref, inner_ref, dz_ref, du_ref, dattn_ref):
    sums_ref[2] += lanes_sum(grad * unit_two)
    sums_ref[3] += lanes_sum(grad)
    grad_summed = normed_back(grad, unit_two, rstd_two, col_ref[:, 2:3])
    dz = grad_summed.astype(BF)
    dz_ref[...] = dz
    du = (dg(wback_ref[...], dz, 0, 0) * slope).astype(BF)
    du_ref[...] = du
    grad_middle = grad_summed + dg(win_ref[...], du, 1, 0)
    sums_ref[0] += lanes_sum(grad_middle * unit_one)
    sums_ref[1] += lanes_sum(grad_middle)
    grad_joined = normed_back(grad_middle, unit_one, rstd_one, col_ref[:, 0:1])
    joined_ref[...] = grad_joined
    dattn = grad_joined.astype(BF)
    dattn_ref[...] = dattn
    grad_ctx = dg(wo_ref[...], dattn, 1, 0)
    for h in range(HEADS):
        rows = slice(h * HEAD_DIM, (h + 1) * HEAD_DIM)
        part = (grad_ctx[rows] * stat_ref[h, 0:1, :]).astype(BF)
        gctx_ref[rows, :] = part
        inner_ref[h] = jnp.sum(part.astype(F32) * ctx[rows].astype(F32), axis=0, keepdims=True)


def first_dense_kernel(act_ref, ctx_ref, wo_ref, win_ref, wback_ref, col_ref, bin_ref,
                       unit_one_ref, unit_two_ref, rstd_ref, low_out_ref, act_out_ref, slope_ref):
    unit_one, rstd_one, _, slope, act, unit_two, rstd_two = dense_forward(
        act_ref[...].astype(F32), ctx_ref[...], wo_ref, win_ref, wback_ref, col_ref, bin_ref)
    unit_one_ref[...] = unit_one
    unit_two_ref[...] = unit_two
    rstd_ref[0:1, :] = rstd_one
    rstd_ref[1:2, :] = rstd_two
    act_out_ref[...] = act
    slope_ref[...] = slope.astype(BF)
    low_out_ref[...] = (unit_two * col_ref[:, 2:3] + col_ref[:, 3:4]).astype(BF)


def tile(rows):
    return pl.BlockSpec((rows, TILE), lambda i: (0, i))


def heads_tile(heads, rows):
    return pl.BlockSpec((heads, rows, TILE), lambda i: (0, 0, i))


def first_dense(act, ctx, w_o, w_in, w_back, columns, bias_in):
    width, tokens = act.shape
    hidden = w_in.shape[1]
    return pl.pallas_call(
        first_dense_kernel,
        name="first_dense",
        grid=(tokens // TILE,),
        in_specs=[tile(width), tile(width), whole(w_o.shape), whole(w_in.shape), whole(w_back.shape), whole(columns.shape), whole(bias_in.shape)],
        out_specs=[tile(width), tile(width), tile(8), tile(width), tile(hidden), tile(hidden)],
        out_shape=[
            jax.ShapeDtypeStruct((width, tokens), F32),
            jax.ShapeDtypeStruct((width, tokens), F32),
            jax.ShapeDtypeStruct((8, tokens), F32),
            jax.ShapeDtypeStruct((width, tokens), BF),
            jax.ShapeDtypeStruct((hidden, tokens), BF),
            jax.ShapeDtypeStruct((hidden, tokens), BF),
        ],
        compiler_params=params(),
        cost_estimate=cost(2 * tokens * width * (width + 2 * hidden), 24 << 20, tokens * hidden),
    )(act, ctx, w_o, w_in, w_back, columns, bias_in)


def second_dense_kernel(unit_ref, ctx_ref, cot_ref, stat_ref, wo_ref, win_ref, wback_ref, col_ref, bin_ref,
                        out_ref, sums_ref, joined_ref, gctx_ref, inner_ref, mid_ref, act_ref, dz_ref, du_ref, dattn_ref):
    @pl.when(pl.program_id(0) == 0)
    def _():
        sums_ref[...] = jnp.zeros(sums_ref.shape, F32)

    ctx = ctx_ref[...]
    signal = unit_ref[...] * col_ref[:, 2:3] + col_ref[:, 3:4]
    unit_one, rstd_one, low_middle, slope, act, unit_two, rstd_two = dense_forward(
        signal, ctx, wo_ref, win_ref, wback_ref, col_ref, bin_ref)
    mid_ref[...] = low_middle
    act_ref[...] = act
    out_ref[...] = (unit_two * col_ref[:, 2:3] + col_ref[:, 3:4]).astype(BF).T
    dense_back(cot_ref[...].astype(F32), unit_one, rstd_one, slope, unit_two, rstd_two, ctx, stat_ref,
               wo_ref, win_ref, wback_ref, col_ref, sums_ref, joined_ref, gctx_ref, inner_ref, dz_ref, du_ref, dattn_ref)


def second_dense(unit, ctx, cot, stat, w_o, w_in, w_back, columns, bias_in):
    width, tokens = unit.shape
    hidden = w_in.shape[1]
    heads = stat.shape[0]
    return pl.pallas_call(
        second_dense_kernel,
        name="second_dense",
        grid=(tokens // TILE,),
        in_specs=[tile(width), tile(width), tile(width), heads_tile(heads, 2),
                  whole(w_o.shape), whole(w_in.shape), whole(w_back.shape), whole(columns.shape), whole(bias_in.shape)],
        out_specs=[pl.BlockSpec((TILE, width), lambda i: (i, 0)), whole((4, width, 128)), tile(width), tile(width), heads_tile(heads, 1),
                   tile(width), tile(hidden), tile(width), tile(hidden), tile(width)],
        out_shape=[
            jax.ShapeDtypeStruct((tokens, width), BF),
            jax.ShapeDtypeStruct((4, width, 128), F32),
            jax.ShapeDtypeStruct((width, tokens), F32),
            jax.ShapeDtypeStruct((width, tokens), BF),
            jax.ShapeDtypeStruct((heads, 1, tokens), F32),
            jax.ShapeDtypeStruct((width, tokens), BF),
            jax.ShapeDtypeStruct((hidden, tokens), BF),
            jax.ShapeDtypeStruct((width, tokens), BF),
            jax.ShapeDtypeStruct((hidden, tokens), BF),
            jax.ShapeDtypeStruct((width, tokens), BF),
        ],
        compiler_params=params(),
        cost_estimate=cost(4 * tokens * width * (width + 2 * hidden), 28 << 20, tokens * hidden),
    )(unit, ctx, cot, stat, w_o, w_in, w_back, columns, bias_in)


def first_back_kernel(prior_ref, dqkv_ref, unit_one_ref, unit_two_ref, rstd_ref, slope_ref, ctx_ref, stat_ref, sums_in_ref,
                      wqkv_ref, wo_ref, win_ref, wback_ref, col_ref,
                      sums_ref, joined_ref, gctx_ref, inner_ref, mid_ref, dz_ref, du_ref, dattn_ref):
    @pl.when(pl.program_id(0) == 0)
    def _():
        sums_ref[...] = sums_in_ref[...]

    unit_one = unit_one_ref[...]
    mid_ref[...] = (unit_one * col_ref[:, 0:1] + col_ref[:, 1:2]).astype(BF)
    grad = prior_ref[...] + dg(wqkv_ref[...], dqkv_ref[...], 1, 0)
    dense_back(grad, unit_one, rstd_ref[0:1, :], slope_ref[...].astype(F32), unit_two_ref[...], rstd_ref[1:2, :], ctx_ref[...], stat_ref,
               wo_ref, win_ref, wback_ref, col_ref, sums_ref, joined_ref, gctx_ref, inner_ref, dz_ref, du_ref, dattn_ref)


def first_back(prior, dqkv, unit_one, unit_two, rstd, slope, ctx, stat, sums, w_qkv, w_o, w_in, w_back, columns):
    width, tokens = prior.shape
    hidden = w_in.shape[1]
    heads = stat.shape[0]
    return pl.pallas_call(
        first_back_kernel,
        name="first_back",
        grid=(tokens // TILE,),
        in_specs=[tile(width), tile(3 * width), tile(width), tile(width), tile(8), tile(hidden), tile(width), heads_tile(heads, 2), whole(sums.shape),
                  whole(w_qkv.shape), whole(w_o.shape), whole(w_in.shape), whole(w_back.shape), whole(columns.shape)],
        out_specs=[whole((4, width, 128)), tile(width), tile(width), heads_tile(heads, 1), tile(width), tile(width), tile(hidden), tile(width)],
        out_shape=[
            jax.ShapeDtypeStruct((4, width, 128), F32),
            jax.ShapeDtypeStruct((width, tokens), F32),
            jax.ShapeDtypeStruct((width, tokens), BF),
            jax.ShapeDtypeStruct((heads, 1, tokens), F32),
            jax.ShapeDtypeStruct((width, tokens), BF),
            jax.ShapeDtypeStruct((width, tokens), BF),
            jax.ShapeDtypeStruct((hidden, tokens), BF),
            jax.ShapeDtypeStruct((width, tokens), BF),
        ],
        compiler_params=params(),
        cost_estimate=cost(2 * tokens * width * (4 * width + 2 * hidden), 28 << 20),
    )(prior, dqkv, unit_one, unit_two, rstd, slope, ctx, stat, sums, w_qkv, w_o, w_in, w_back, columns)


def weight_kernel(la_ref, lb_ref, ra_ref, rb_ref, out_ref, sum_ref):
    ra, rb = ra_ref[...], rb_ref[...]
    out_ref[...] = (dg(la_ref[...], ra, 1, 1) + dg(lb_ref[...], rb, 1, 1)).astype(BF)
    ones = jnp.ones((16, ra.shape[1]), BF)
    sum_ref[...] = (dg(ones, ra, 1, 1) + dg(ones, rb, 1, 1))[0:8]


def weight_grad(left_one, left_two, right_one, right_two, block):
    rows, tokens = left_one.shape
    columns = right_one.shape[0]
    return pl.pallas_call(
        weight_kernel,
        name="weight_grad",
        grid=(columns // block,),
        in_specs=[whole((rows, tokens)), whole((rows, tokens)), pl.BlockSpec((block, tokens), lambda i: (i, 0)), pl.BlockSpec((block, tokens), lambda i: (i, 0))],
        out_specs=[pl.BlockSpec((rows, block), lambda i: (0, i)), pl.BlockSpec((8, block), lambda i: (0, i))],
        out_shape=[jax.ShapeDtypeStruct((rows, columns), BF), jax.ShapeDtypeStruct((8, columns), F32)],
        compiler_params=params(),
        cost_estimate=cost(4 * rows * columns * tokens, 4 * (rows + columns) * tokens + 2 * rows * columns),
    )(left_one, left_two, right_one, right_two)


def input_kernel(joined_ref, dqkv_ref, wqkv_ref, out_ref):
    out_ref[...] = (joined_ref[...] + dg(wqkv_ref[...], dqkv_ref[...], 1, 0)).T


def input_gradient(joined, dqkv, w_qkv):
    width, tokens = joined.shape
    return pl.pallas_call(
        input_kernel,
        name="input_gradient",
        grid=(tokens // TILE,),
        in_specs=[tile(width), tile(3 * width), whole(w_qkv.shape)],
        out_specs=pl.BlockSpec((TILE, width), lambda i: (i, 0)),
        out_shape=jax.ShapeDtypeStruct((tokens, width), F32),
        compiler_params=params(),
        cost_estimate=cost(6 * width * width * tokens, 8 << 20),
    )(joined, dqkv, w_qkv)


def masks(segments, tags, length):
    tokens = segments.shape[0]
    matches = segments[None, :] == jnp.arange(tags.shape[0], dtype=jnp.int32)[:, None]
    group = jnp.sum(jnp.where(matches, tags[:, None], 0), axis=0)
    live = jnp.arange(tokens, dtype=jnp.int32) < length
    kinds = jnp.arange(16, dtype=jnp.int32)[:, None]
    same = group[None, :] == kinds
    kmask = jnp.where(kinds < 4, (same & live[None, :]).astype(F32), jnp.where(kinds == 4, (~live)[None, :].astype(F32), 0.0))
    qmask = jnp.where(kinds < 4, jnp.where(same, 0.0, -FAR), jnp.where(kinds == 4, -FAR, 0.0))
    return kmask.astype(BF), jnp.broadcast_to(qmask, (16, tokens)).astype(BF)


def on_device(inputs, cotangent, lengths, segment_ids, group_tags, weights, first_moments, second_moments, vectors, vector_first, vector_second):
    row_count, tokens, width = inputs.shape
    matrices = lax.all_gather(weights.astype(BF), "shard", axis=0, tiled=True)
    low_vectors = lax.all_gather(vectors.astype(BF), "shard", axis=1, tiled=True)
    vector_rows = low_vectors.astype(F32)
    columns = vector_rows.T
    bias_in = vector_rows[8:].reshape(FF, 1)
    w_qkv = matrices[:, : 3 * D]
    w_o = matrices[:, 3 * D : 4 * D]
    w_in = matrices[:, 4 * D : 4 * D + FF]
    w_back = matrices[:, 4 * D + FF :]
    bias_q, bias_v = columns[:, 4:5], columns[:, 5:6]
    kmask, qmask = masks(segment_ids[0], group_tags[0], lengths[0])
    act_one = inputs[0].T
    cot = cotangent[0].T

    e_one, ctx_one, qkv_one, stat_one = attend(act_one, w_qkv, bias_q, bias_v, kmask, qmask)
    unit_one, unit_two, rstd, act_two, hid_one, slope = first_dense(act_one, ctx_one, w_o, w_in, w_back, columns, bias_in)
    e_two, ctx_two, qkv_two, stat_two = attend(act_two, w_qkv, bias_q, bias_v, kmask, qmask)
    outputs, sums, joined_two, gctx_two, inner_two, mid_two, hid_two, dz_two, du_two, dattn_two = second_dense(
        unit_two, ctx_two, cot, stat_two, w_o, w_in, w_back, columns, bias_in)
    dqkv_two = attend_back(e_two, qkv_two, stat_two, gctx_two, inner_two).reshape(3 * width, tokens)
    sums, joined_one, gctx_one, inner_one, mid_one, dz_one, du_one, dattn_one = first_back(
        joined_two, dqkv_two, unit_one, unit_two, rstd, slope, ctx_one, stat_one, sums, w_qkv, w_o, w_in, w_back, columns)
    grad_in, sum_in = weight_grad(mid_one, mid_two, du_one, du_two, 512)
    grad_back, _ = weight_grad(dz_one, dz_two, hid_one, hid_two, 512)
    grad_o, sum_o = weight_grad(ctx_one, ctx_two, dattn_one, dattn_two, 512)
    dqkv_one = attend_back(e_one, qkv_one, stat_one, gctx_one, inner_one).reshape(3 * width, tokens)
    grad_qkv, sum_qkv = weight_grad(act_one, act_two, dqkv_one, dqkv_two, 512)
    input_grad = input_gradient(joined_one, dqkv_one, w_qkv)
    sum_back = jnp.sum(dz_one.astype(F32), axis=1) + jnp.sum(dz_two.astype(F32), axis=1)
    small = jnp.sum(sums, axis=2)
    vector_grad = jnp.concatenate(
        [small, sum_qkv[0:1, :width], sum_qkv[0:1, 2 * width :], sum_o[0:1], sum_back[None], sum_in[0].reshape(FF // width, width)], axis=0)
    weight_grads = jnp.concatenate([grad_qkv, grad_o, grad_in, grad_back], axis=1)

    own_weight = lax.psum_scatter(weight_grads, "shard", scatter_dimension=0, tiled=True)
    own_vector = lax.psum_scatter(vector_grad.astype(BF), "shard", scatter_dimension=1, tiled=True)
    own_weight = lax.psum(own_weight, "batch").astype(F32)
    own_vector = lax.psum(own_vector, "batch").astype(F32)
    squares = lax.psum(jnp.sum(own_weight * own_weight) + jnp.sum(own_vector * own_vector), "shard")
    grad_norm = jnp.sqrt(squares)
    clip_limit = math.sqrt(D * WCOLS)
    factor = clip_limit / jnp.maximum(grad_norm, clip_limit)
    new_weights, new_first, new_second = adam_update(weights, first_moments, second_moments, own_weight * factor)
    new_vectors, new_vector_first, new_vector_second = adam_update(vectors, vector_first, vector_second, own_vector * factor)
    return (
        outputs[None],
        input_grad[None],
        own_weight,
        own_vector,
        grad_norm,
        new_weights,
        new_first,
        new_second,
        new_vectors,
        new_vector_first,
        new_vector_second,
    )


def solution(mesh):
    rows = ("batch", "shard")
    placed = (
        P(rows, None, None),
        P(rows, None, None),
        P(rows),
        P(rows, None),
        P(rows, None),
        P("shard", None),
        P("shard", None),
        P("shard", None),
        P(None, "shard"),
        P(None, "shard"),
        P(None, "shard"),
    )
    return jax.shard_map(
        on_device,
        mesh=mesh,
        in_specs=placed,
        out_specs=(
            P(rows, None, None),
            P(rows, None, None),
            P("shard", None),
            P(None, "shard"),
            P(),
            P("shard", None),
            P("shard", None),
            P("shard", None),
            P(None, "shard"),
            P(None, "shard"),
            P(None, "shard"),
        ),
        check_vma=False,
    )
```

time: 719 us -> 564 us (0.78)
  matrix products: 250 us -> 0 us
  Pallas kernels: 0 us -> 185 us
  other arithmetic: 104 us -> 22.4 us
  local copies, waits for them, and re-layouts: 30.2 us -> 18.6 us
    dot_general x48 -> x0, matrix products: 250 us -> none  [the longest x4 41.6 us: attend_backward(): jnp.einsum('qhd,khd->hqk', grad_block, values, preferred_element_type=jnp...]
    pallas_call x0 -> x12, Pallas kernels: none -> 185 us  [the longest x2 42.8 us: attend_back(): pl.pallas_call(attend_back_kernel, name='attend_back', grid=(pairs,), in_...]
    convert_element_type x9 -> x3, other arithmetic: 53.6 us -> 4 us  [the longest x1 3.3 us: on_device(): matrices = lax.all_gather(weights.astype(BF), 'shard', axis=0, tiled=True)]
    reduce_sum x20 -> x4, other arithmetic: 30.4 us -> 0.85 us  [the longest x1 0.35 us: on_device(): small = jnp.sum(sums, axis=2)]
    unnamed x196 -> x38, local copies, waits for them, and re-layouts: 19.2 us -> 6.08 us
    slice x5 -> x9, local copies, waits for them, and re-layouts: 0.16 us -> 12.3 us  [the longest x1 4.82 us: on_device(): w_back = matrices[:, 4 * D + FF:]]
    convert_element_type x2 -> x1, local copies, waits for them, and re-layouts: 8.05 us -> 0.13 us  [on_device(): vectors.astype(BF)]
where the time goes in v1:
time: 564 us; the launch traced here: 555 us
  waiting for transfers between devices  271 us (48%)
  Pallas kernels  185 us (33%)
  blocking collectives  39.3 us (7%)
  other arithmetic  22.4 us (4%)
  local copies, waits for them, and re-layouts  18.6 us (3%)
  between operations  18.3 us (3%)
    reduce_scatter x1, waiting for transfers between devices, on_device(): lax.psum_scatter(weight_grads, 'shard', scatter_dimension=0, tiled=True)  105 us
    all_gather x1, waiting for transfers between devices, on_device(): matrices = lax.all_gather(weights.astype(BF), 'shard', axis=0, tiled=True)  96.1 us
    psum x1, waiting for transfers between devices, on_device(): own_weight = lax.psum(own_weight, 'batch').astype(F32)  47.3 us
    pallas_call x2, Pallas kernels, attend_back(): pl.pallas_call(attend_back_kernel, name='attend_back', grid=(pairs,), in_...  42.8 us
    pallas_call x2, Pallas kernels, attend(): pl.pallas_call(attend_kernel, name='attend', grid=(pairs,), in_specs=[who...  36.3 us
    pallas_call x4, Pallas kernels, weight_grad(): pl.pallas_call(weight_kernel, name='weight_grad', grid=(columns // block,...  32.7 us
    pallas_call x1, Pallas kernels, second_dense(): pl.pallas_call(second_dense_kernel, name='second_dense', grid=(tokens //...  29.4 us
    unnamed x5, waiting for transfers between devices  22.6 us
  transfers between devices with their start and end apart: 4, of which 4 were waited for; matrix products, arithmetic and copies ran while one was open for 2% of the time, Pallas kernels for 0%

profile of v1, /device:TPU:0, one launch (start us, length us, event | category | flops | bytes accessed | tf_op | source)
XLA Modules:
  0.0 555.3 jit_solution(8856664676912792075)
XLA Ops:
  7.2 3.3 convert_element_type.39
  10.6 0.0 reduce-scatter.5.cloned.1.call-start
  11.4 0.1 copy.44
  11.5 15.1 %all_gather.7 = bf16[12,512]{0,1:T(8,128)(2,1)S(1)} all-gather(bf16[12,128]{0,1:T(8,128)(2,1)S(1)} %copy.44), channel_id=1, replica_groups=mesh['batch'=8,'shard'=4] {'shard'}, dimensions={1}, use_global_device_ids=true | all-gather | bytes 15360 | tf_op jit(solution)/shard_map/all_gather | solution.py:446
  26.6 0.1 slice.54
  26.7 0.1 copy.45
  26.8 1.3 copy.52
  28.2 1.3 copy.43
  29.5 1.3 copy.47
  30.9 0.1 select_reduce_fusion
  31.0 0.7 select_convert_fusion
  31.7 1.0 fusion.7
  32.7 96.1 %all-gather.2.cloned.1.call-done = bf16[512,6144]{1,0:T(8,128)(2,1)} async-done(((bf16[128,6144]{1,0:T(8,128)(2,1)}), bf16[512,6144]{1,0:T(8,128)(2,1)}) %all-gather.2.cloned.1.call-update) | async-done | bytes 6291472 | tf_op jit(solution)/shard_map/all_gather | solution.py:445
  128.8 2.6 slice.48.wq_ref.wk_ref.wv_ref.wqkv_ref
  131.5 21.2 %attend.2 = (bf16[8,1024,1024]{2,1,0:T(8,128)(2,1)}, bf16[512,1024]{1,0:T(8,128)(2,1)}, bf16[3,512,1024]{2,1,0:T(8,128)(2,1)}, f32[8,2,1024]{2,1,0:T(2,128)}) custom-call(bf16[512,1024]{1,0:T(8,128)(2,1)} %bitcast.27, bf16[512,1536]{1,0:T(8,128)(2,1)} %slice.48.wq_ref.wk_ref.wv_ref.wqkv_ref, bf16[512,1536]{1,0:T(8,128)(2,1)} %slice.48.wq_ref.wk_ref.wv_ref.wqkv_ref, ...), custom_call_target="tpu_custom_call" | custom-call | flops 3758096384 | bytes 16777216 | tf_op jit(solution)/shard_map/attend/pallas_call | solution.py:122
  152.6 1.9 slice.51.wo_ref
  154.5 4.8 fusion.6
  159.3 17.9 %first_dense.1 = (f32[512,1024]{1,0:T(8,128)}, f32[512,1024]{1,0:T(8,128)}, f32[8,1024]{1,0:T(8,128)}, bf16[512,1024]{1,0:T(8,128)(2,1)}, bf16[2048,1024]{1,0:T(8,128)(2,1)}, /*index=5*/bf16[2048,1024]{1,0:T(8,128)(2,1)}) custom-call(bf16[512,1024]{1,0:T(8,128)(2,1)} %bitcast.28, bf16[512,1024]{1,0:T(8,128)(2,1)} %get-tuple-element.50.ctx_ref.la_ref, ...), custom_call_target="tpu_custom_call" | custom-call | flops 4831838208 | bytes 25165824 | tf_op jit(solution)/shard_map/first_dense/pallas_call | solution.py:286
  177.2 15.2 %attend.3 = (bf16[8,1024,1024]{2,1,0:T(8,128)(2,1)}, bf16[512,1024]{1,0:T(8,128)(2,1)}, bf16[3,512,1024]{2,1,0:T(8,128)(2,1)}, f32[8,2,1024]{2,1,0:T(2,128)}) custom-call(bf16[512,1024]{1,0:T(8,128)(2,1)} %get-tuple-element.52.act_ref.lb_ref, bf16[512,1536]{1,0:T(8,128)(2,1)} %slice.48.wq_ref.wk_ref.wv_ref.wqkv_ref, ...), custom_call_target="tpu_custom_call" | custom-call | flops 3758096384 | bytes 16777216 | tf_op jit(solution)/shard_map/attend/pallas_call | solution.py:122
  192.4 29.4 %second_dense.1 = (bf16[1024,512]{1,0:T(8,128)(2,1)}, f32[4,512,128]{2,1,0:T(8,128)}, f32[512,1024]{1,0:T(8,128)}, bf16[512,1024]{1,0:T(8,128)(2,1)}, f32[8,1,10...) custom-call(f32[512,1024]{1,0:T(8,128)} %get-tuple-element.51.unit_r, ...), custom_call_target="tpu_custom_call" | custom-call | flops 9663676416 | bytes 29360128 | tf_op jit(solution)/shard_map/second_dense/pallas_call | solution.py:326
  221.8 21.5 %attend_back.2 = bf16[3,512,1024]{2,1,0:T(8,128)(2,1)} custom-call(bf16[8,1024,1024]{2,1,0:T(8,128)(2,1)} %get-tuple-element.57.e_ref, bf16[3,512,1024]{2,1,0:T(8,128)(2,1)} %get-tuple-element.58.qkv_ref, f32[8,2,1024]{2,1,0:T(2,128)} %get-tuple-element.54.stat_ref, bf16[512,1024]{1,0:T(8,128)(2,1)} %get-tuple-element.59.grad_ref, ...), custom_call_target="tpu_custom_call" | custom-call | flops 4294967296 | bytes 16777216 | tf_op jit(solution)/shard_map/attend_back/pallas_call | solution.py:175
  243.3 19.9 %first_back.1 = (f32[4,512,128]{2,1,0:T(8,128)}, f32[512,1024]{1,0:T(8,128)}, bf16[512,1024]{1,0:T(8,128)(2,1)}, f32[8,1,1024]{2,1,0:T(1,128)}, bf16[512,1024]{1...) custom-call(f32[512,1024]{1,0:T(8,128)} %get-tuple-element.56.prior_ref, ...), custom_call_target="tpu_custom_call" | custom-call | flops 6442450944 | bytes 29360128 | tf_op jit(solution)/shard_map/first_back/pallas_call | solution.py:369
  263.3 21.3 %attend_back.3 = bf16[3,512,1024]{2,1,0:T(8,128)(2,1)} custom-call(bf16[8,1024,1024]{2,1,0:T(8,128)(2,1)} %get-tuple-element.67.e_ref, bf16[3,512,1024]{2,1,0:T(8,128)(2,1)} %get-tuple-element.68.qkv_ref, f32[8,2,1024]{2,1,0:T(2,128)} %get-tuple-element.64.stat_ref, bf16[512,1024]{1,0:T(8,128)(2,1)} %get-tuple-element.69.grad_ref, ...), custom_call_target="tpu_custom_call" | custom-call | flops 4294967296 | bytes 16777216 | tf_op jit(solution)/shard_map/attend_back/pallas_call | solution.py:175
  284.6 8.1 %weight_grad.4 = (bf16[512,1536]{1,0:T(8,128)(2,1)}, f32[8,1536]{1,0:T(8,128)}) custom-call(bf16[512,1024]{1,0:T(8,128)(2,1)} %bitcast.29, bf16[512,1024]{1,0:T(8,128)(2,1)} %get-tuple-element.52.act_ref.lb_ref, bf16[1536,1024]{1,0:T(8,128)(2,1)} %bitcast.22, bf16[1536,1024]{1,0:T(8,128)(2,1)} %bitcast.25), custom_call_target="tpu_custom_call" | custom-call | flops 3221225472 | bytes 9961472 | tf_op jit(solution)/shard_map/weight_grad/pallas_call | solution.py:401
  292.6 4.5 weight_grad.5
  297.2 10.1 %weight_grad.7 = (bf16[512,2048]{1,0:T(8,128)(2,1)}, f32[8,2048]{1,0:T(8,128)}) custom-call(bf16[512,1024]{1,0:T(8,128)(2,1)} %get-tuple-element.80.la_ref, bf16[512,1024]{1,0:T(8,128)(2,1)} %get-tuple-element.81.lb_ref, bf16[2048,1024]{1,0:T(8,128)(2,1)} %get-tuple-element.82.ra_ref, bf16[2048,1024]{1,0:T(8,128)(2,1)} %get-tuple-element.83.rb_ref), custom_call_target="tpu_custom_call" | custom-call | flops 4294967296 | bytes 12582912 | tf_op jit(solution)/shard_map/weight_grad/pallas_call | solution.py:401
  307.2 10.0 %weight_grad.6 = (bf16[512,2048]{1,0:T(8,128)(2,1)}, f32[8,2048]{1,0:T(8,128)}) custom-call(bf16[512,1024]{1,0:T(8,128)(2,1)} %get-tuple-element.75.la_ref, bf16[512,1024]{1,0:T(8,128)(2,1)} %get-tuple-element.76.lb_ref, bf16[2048,1024]{1,0:T(8,128)(2,1)} %get-tuple-element.77.ra_ref, bf16[2048,1024]{1,0:T(8,128)(2,1)} %get-tuple-element.78.rb_ref), custom_call_target="tpu_custom_call" | custom-call | flops 4294967296 | bytes 12582912 | tf_op jit(solution)/shard_map/weight_grad/pallas_call | solution.py:401
  317.2 5.0 pad_maximum_fusion
  322.2 0.0 reduce-scatter.7.cloned.1.call-start
  322.3 0.9 slice.63
  323.2 0.3 copy-done.6
  323.4 0.2 convert_reduce_fusion
  323.7 0.1 copy-done.8
  323.8 0.2 convert_reduce_fusion.1
  324.0 0.9 fusion.3
  324.9 0.4 reduce_sum.55
  325.3 0.8 copy.49
  326.2 105.2 %reduce-scatter.5.cloned.1.call-done = bf16[128,6144]{1,0:T(8,128)(2,1)} async-done(((bf16[512,6144]{1,0:T(8,128)(2,1)}), bf16[128,6144]{1,0:T(8,128)(2,1)}) %reduce-scatter.5.cloned.1.call-update) | async-done | bytes 1572880 | tf_op jit(solution)/shard_map/reduce_scatter | solution.py:479
  431.4 22.5 %reduce-scatter.7.cloned.1.call-done = bf16[128,12]{1,0:T(8,128)(2,1)} async-done(((bf16[512,12]{1,0:T(8,128)(2,1)}), bf16[128,12]{1,0:T(8,128)(2,1)}) %reduce-scatter.7.cloned.1.call-update) | async-done | bytes 3088
  453.9 0.8 copy.50
  454.7 11.9 %psum.22 = bf16[12,128]{1,0:T(8,128)(2,1)S(1)} all-reduce(bf16[12,128]{1,0:T(8,128)(2,1)S(1)} %copy.50), channel_id=1, replica_groups=mesh['batch'=8,'shard'=4] {'batch'}, use_global_device_ids=true, to_apply=%region_7.8 | all-reduce | flops 1536 | bytes 6144 | tf_op jit(solution)/shard_map/psum | solution.py:482
  466.7 0.6 multiply_reduce_fusion.1
  467.3 47.3 %all-reduce.2.cloned.1.call-done = bf16[128,6144]{1,0:T(8,128)(2,1)} async-done(((bf16[128,6144]{1,0:T(8,128)(2,1)}), bf16[128,6144]{1,0:T(8,128)(2,1)}) %all-reduce.2.cloned.1.call-update) | async-done | bytes 1572880 | tf_op jit(solution)/shard_map/psum | solution.py:481
  514.6 4.4 multiply_reduce_fusion
  520.3 6.3 %input_gradient.1 = f32[1024,512]{1,0:T(8,128)} custom-call(f32[512,1024]{1,0:T(8,128)} %get-tuple-element.66.joined_ref, bf16[1536,1024]{1,0:T(8,128)(2,1)} %bitcast.23, bf16[512,1536]{1,0:T(8,128)(2,1)} %slice.48.wq_ref.wk_ref.wv_ref.wqkv_ref), custom_call_target="tpu_custom_call" | custom-call | flops 1610612736 | bytes 8388608 | tf_op jit(solution)/shard_map/input_gradient/pallas_call | solution.py:419
  526.6 12.3 %psum.23 = f32[]{:T(128)} all-reduce(f32[]{:T(128)S(6)} %add.58), channel_id=1, replica_groups=mesh['batch'=8,'shard'=4] {'shard'}, use_global_device_ids=true, to_apply=%region_10.11 | all-reduce | flops 1 | bytes 8 | tf_op jit(solution)/shard_map/psum | solution.py:483
  539.7 0.6 multiply_subtract_fusion.1
  540.4 6.9 %multiply_subtract_fusion = (f32[128,6144]{1,0:T(8,128)}, f32[128,6144]{1,0:T(8,128)}, f32[128,6144]{1,0:T(8,128)}) fusion(f32[128,6144]{1,0:T(8,128)S(1)} %copy-done, f32[128,6144]{1,0:T(8,128)} %get-tuple-element.98, f32[]{:T(128)S(6)} %div.21, f32[128,6144]{1,0:T(8,128)} %param.17, f32[128,6144]{1,0:T(8,128)} %param.18), kind=kLoop, calls=%fused_computation.4 | loop fusion | flops 11796480 | bytes 22020100 | tf_op jit(solution)/shard_map/sub | solution.py:58
  (48 shorter events, 0.4 us)
Async XLA Ops:
  7.2 4.2 copy-start.10
  7.2 21.0 %copy-start.4 = (bf16[1,1024,512]{2,1,0:T(8,128)(2,1)S(1)}, bf16[1,1024,512]{2,1,0:T(8,128)(2,1)}, u32[]{:S(2)}) copy-start(bf16[1,1024,512]{2,1,0:T(8,128)(2,1)} %param.11) | copy-start | bytes 3145732
  7.2 121.6 %all-gather.2.cloned.1.call-start = ((), (), s32[]{:S(2)}) async-start(), calls=%async_computation.2 | async-start | bytes 7864320 | tf_op jit(solution)/shard_map/all_gather | solution.py:445
  10.5 19.0 %copy-start.5 = (bf16[1,1024,512]{2,1,0:T(8,128)(2,1)S(1)}, bf16[1,1024,512]{2,1,0:T(8,128)(2,1)}, u32[]{:S(2)}) copy-start(bf16[1,1024,512]{2,1,0:T(8,128)(2,1)} %param.12) | copy-start | bytes 3145732
  10.6 420.8 %reduce-scatter.5.cloned.1.call-start = ((), (), s32[]{:S(2)}) async-start(), calls=%async_computation.3 | async-start | bytes 7864320 | tf_op jit(solution)/shard_map/reduce_scatter | solution.py:479
  11.4 19.5 %copy-start.14 = (s32[1,1024]{1,0:T(1,128)S(1)}, s32[1,1024]{1,0:T(1,128)}, u32[]{:S(2)}) copy-start(s32[1,1024]{1,0:T(1,128)} %param.14) | copy-start | bytes 12292
  11.4 19.5 %copy-start.15 = (s32[1,8]{1,0:T(1,128)S(1)}, s32[1,8]{1,0:T(1,128)}, u32[]{:S(2)}) copy-start(s32[1,8]{1,0:T(1,128)} %param.15) | copy-start | bytes 100
  31.7 120.9 %copy-start.1 = (f32[512,12]{1,0:T(8,128)}, f32[512,12]{1,0:T(8,128)S(1)}, u32[]{:S(2)}) copy-start(f32[512,12]{1,0:T(8,128)S(1)} %convert_bitcast_fusion.col_ref) | copy-start | bytes 73732
  307.2 10.0 %copy-start.2 = (bf16[512,2048]{1,0:T(8,128)(2,1)S(1)}, bf16[512,2048]{1,0:T(8,128)(2,1)}, u32[]{:S(2)}) copy-start(bf16[512,2048]{1,0:T(8,128)(2,1)} %get-tuple-element.84) | copy-start | bytes 6291460
  307.2 10.0 %copy-start.3 = (bf16[512,1536]{1,0:T(8,128)(2,1)S(1)}, bf16[512,1536]{1,0:T(8,128)(2,1)}, u32[]{:S(2)}) copy-start(bf16[512,1536]{1,0:T(8,128)(2,1)} %get-tuple-element.71) | copy-start | bytes 4718596
  322.2 1.2 copy-start.6
  322.2 1.6 copy-start.8
  322.2 2.7 copy-start.9
  322.2 2.7 copy-start.7
  322.2 131.7 %reduce-scatter.7.cloned.1.call-start = ((), (), s32[]{:S(2)}) async-start(), calls=%async_computation.5 | async-start | bytes 163840
  326.1 188.4 %all-reduce.2.cloned.1.call-start = ((), (), s32[]{:S(2)}) async-start(), calls=%async_computation.4 | async-start | bytes 3145728 | tf_op jit(solution)/shard_map/psum | solution.py:481
  467.3 72.4 %copy-start.11 = (f32[12,128]{1,0:T(8,128)}, f32[12,128]{1,0:T(8,128)S(1)}, u32[]{:S(2)}) copy-start(f32[12,128]{1,0:T(8,128)S(1)} %get-tuple-element.96) | copy-start | bytes 18436
  520.3 19.4 %copy-start.12 = (f32[12,128]{1,0:T(8,128)S(1)}, f32[12,128]{1,0:T(8,128)}, u32[]{:S(2)}) copy-start(f32[12,128]{1,0:T(8,128)} %param.20) | copy-start | bytes 18436
  520.3 19.4 %copy-start.13 = (f32[12,128]{1,0:T(8,128)S(1)}, f32[12,128]{1,0:T(8,128)}, u32[]{:S(2)}) copy-start(f32[12,128]{1,0:T(8,128)} %param.21) | copy-start | bytes 18436
  520.3 20.1 %copy-start = (f32[128,6144]{1,0:T(8,128)S(1)}, f32[128,6144]{1,0:T(8,128)}, u32[]{:S(2)}) copy-start(f32[128,6144]{1,0:T(8,128)} %param.16) | copy-start | bytes 9437188
Sparse Core Ops, SparseCore 0:
  10.7 118.0 all-gather.1
  322.4 108.9 reduce-scatter.4
  434.2 19.6 reduce-scatter.6
  457.4 57.1 all-reduce.1

commit v2 on v1

v2 whole, which is shorter than its diff:
```python
import functools
import math

import jax
import jax.numpy as jnp
from jax import lax
from jax.experimental import pallas as pl
from jax.experimental.pallas import tpu as pltpu
from jax.sharding import PartitionSpec as P

D = 512
FF = 2048
HEADS = 8
HEAD_DIM = 64
STEP = 10
WCOLS = 6144

NORM_EPS = 1e-05
BETA_ONE = 0.5
BETA_TWO = 0.5
ADAM_EPS = 1e-08
DECAY = 0.01
WARMUP = 4000.0
RATE_SCALE = 150000.0

BF = jnp.bfloat16
F32 = jnp.float32
FAR = 1e30
SAFE_SCORE = 60.0
TILE = 256
LANES = 128
VMEM_BYTES = 60 << 20


def params():
    return pltpu.CompilerParams(vmem_limit_bytes=VMEM_BYTES)


def cost(flops, bytes_accessed, transcendentals=0):
    return pl.CostEstimate(flops=int(flops), bytes_accessed=int(bytes_accessed), transcendentals=int(transcendentals))


def dg(left, right, left_dim, right_dim):
    return lax.dot_general(
        left, right, (((left_dim,), (right_dim,)), ((), ())), preferred_element_type=F32
    )


def whole(shape):
    return pl.BlockSpec(shape, lambda i: (0,) * len(shape))


def adam_update(master, moment_one, moment_two, gradient):
    moment_one = BETA_ONE * moment_one + (1.0 - BETA_ONE) * gradient
    moment_two = BETA_TWO * moment_two + (1.0 - BETA_TWO) * gradient * gradient
    step_rate = RATE_SCALE * D ** (-0.5) * min(STEP ** (-0.5), STEP * WARMUP ** (-1.5))
    fixed_first = moment_one / (1.0 - BETA_ONE**STEP)
    fixed_second = moment_two / (1.0 - BETA_TWO**STEP)
    master = master - step_rate * (
        fixed_first / (jnp.sqrt(fixed_second) + ADAM_EPS) + DECAY * master
    )
    return (master, moment_one, moment_two)


def attend_kernel(act_ref, wq_ref, wk_ref, wv_ref, col_ref, kmask_ref, qmask_ref, e_ref, ctx_ref, qkv_ref, stat_ref):
    act = act_ref[...]
    tokens = act.shape[1]
    q = (dg(wq_ref[...], act, 0, 0) + col_ref[:, 4:5].astype(F32)).astype(BF) * jnp.asarray(HEAD_DIM**-0.5, BF)
    k = dg(wk_ref[...], act, 0, 0).astype(BF)
    v = (dg(wv_ref[...], act, 0, 0) + col_ref[:, 5:6].astype(F32)).astype(BF)
    qkv_ref[0] = q
    qkv_ref[1] = k
    qkv_ref[2] = v
    dead = kmask_ref[4:5, :].astype(F32)
    bound = jnp.zeros((1, 1), F32)
    selves = []
    for h in range(2):
        rows = slice(h * HEAD_DIM, (h + 1) * HEAD_DIM)
        qf, kf = q[rows].astype(F32), k[rows].astype(F32)
        selves.append(jnp.sum(qf * kf, axis=0, keepdims=True))
        q_top = jnp.max(jnp.sum(qf * qf, axis=0, keepdims=True), axis=1, keepdims=True)
        k_top = jnp.max(jnp.sum(kf * kf, axis=0, keepdims=True), axis=1, keepdims=True)
        bound = jnp.maximum(bound, q_top * k_top)
    safe = bound[0, 0] <= SAFE_SCORE * SAFE_SCORE

    def scores(h):
        rows = slice(h * HEAD_DIM, (h + 1) * HEAD_DIM)
        keys = jnp.concatenate([k[rows], kmask_ref[...]], axis=0).T
        queries = jnp.concatenate([q[rows], qmask_ref[...]], axis=0)
        return dg(keys, queries, 1, 0)

    def finish(h, e, e_self):
        rows = slice(h * HEAD_DIM, (h + 1) * HEAD_DIM)
        low_e = e.astype(BF)
        e_ref[h] = low_e
        total = jnp.sum(e, axis=0, keepdims=True) + e_self
        scale = 1.0 / total
        values = v[rows]
        mixed = dg(values, low_e, 1, 0) + values.astype(F32) * e_self.astype(BF).astype(F32)
        ctx_ref[rows, :] = (mixed * scale).astype(BF)
        stat_ref[h, 0:1, :] = scale
        stat_ref[h, 1:2, :] = e_self

    @pl.when(safe)
    def _():
        for h in range(2):
            finish(h, jnp.exp(scores(h)), jnp.exp(selves[h]) * dead)

    @pl.when(jnp.logical_not(safe))
    def _():
        for h in range(2):
            s = scores(h)
            own = jnp.where(dead > 0, selves[h], -FAR)
            top = jnp.maximum(jnp.max(s, axis=0, keepdims=True), own)
            finish(h, jnp.exp(s - top), jnp.exp(own - top) * dead)


def attend(act, w_qkv, kmask, qmask):
    width, tokens = act.shape
    pairs = width // (2 * HEAD_DIM)
    pair = 2 * HEAD_DIM
    heads = width // HEAD_DIM
    return pl.pallas_call(
        attend_kernel,
        name="attend",
        grid=(pairs,),
        in_specs=[
            whole((width, tokens)),
            pl.BlockSpec((width, pair), lambda i: (0, i)),
            pl.BlockSpec((width, pair), lambda i: (0, pairs + i)),
            pl.BlockSpec((width, pair), lambda i: (0, 2 * pairs + i)),
            pl.BlockSpec((pair, pair), lambda i: (i, 3 * pairs)),
            whole((16, tokens)),
            whole((16, tokens)),
        ],
        out_specs=[
            pl.BlockSpec((2, tokens, tokens), lambda i: (i, 0, 0)),
            pl.BlockSpec((pair, tokens), lambda i: (i, 0)),
            pl.BlockSpec((3, pair, tokens), lambda i: (0, i, 0)),
            pl.BlockSpec((2, 2, tokens), lambda i: (i, 0, 0)),
        ],
        out_shape=[
            jax.ShapeDtypeStruct((heads, tokens, tokens), BF),
            jax.ShapeDtypeStruct((width, tokens), BF),
            jax.ShapeDtypeStruct((3, width, tokens), BF),
            jax.ShapeDtypeStruct((heads, 2, tokens), F32),
        ],
        compiler_params=params(),
        cost_estimate=cost(6 * width * width * tokens + 4 * width * tokens * tokens, 2 * heads * tokens * tokens, heads * tokens * tokens),
    )(act, w_qkv, w_qkv, w_qkv, w_qkv, kmask, qmask)


def attend_back_kernel(e_ref, qkv_ref, stat_ref, grad_ref, inner_ref, out_ref, ds_ref):
    for h in range(2):
        rows = slice(h * HEAD_DIM, (h + 1) * HEAD_DIM)
        q, k, v = qkv_ref[0, rows], qkv_ref[1, rows], qkv_ref[2, rows]
        grad = grad_ref[rows]
        inner = inner_ref[h]
        e_self = stat_ref[h, 1:2, :]
        grad_f = grad.astype(F32)
        ds = (e_ref[h].astype(F32) * (dg(v.T, grad, 1, 0) - inner)).astype(BF)
        ds_ref[h] = ds
        own = (e_self * (jnp.sum(grad_f * v.astype(F32), axis=0, keepdims=True) - inner)).astype(BF).astype(F32)
        scale = HEAD_DIM**-0.5
        out_ref[0, rows] = ((dg(k, ds, 1, 0) + k.astype(F32) * own) * scale).astype(BF)
        out_ref[2, rows] = (dg(grad, e_ref[h], 1, 1) + grad_f * e_self.astype(BF).astype(F32)).astype(BF)
        out_ref[1, rows] = (dg(q, ds_ref[h], 1, 1) + q.astype(F32) * own).astype(BF)


def attend_back(e, qkv, stat, grad, inner):
    heads, tokens, _ = e.shape
    width = grad.shape[0]
    pairs = heads // 2
    pair = 2 * HEAD_DIM
    return pl.pallas_call(
        attend_back_kernel,
        name="attend_back",
        grid=(pairs,),
        in_specs=[
            pl.BlockSpec((2, tokens, tokens), lambda i: (i, 0, 0)),
            pl.BlockSpec((3, pair, tokens), lambda i: (0, i, 0)),
            pl.BlockSpec((2, 2, tokens), lambda i: (i, 0, 0)),
            pl.BlockSpec((pair, tokens), lambda i: (i, 0)),
            pl.BlockSpec((2, 1, tokens), lambda i: (i, 0, 0)),
        ],
        out_specs=pl.BlockSpec((3, pair, tokens), lambda i: (0, i, 0)),
        out_shape=jax.ShapeDtypeStruct((3, width, tokens), BF),
        scratch_shapes=[pltpu.VMEM((2, tokens, tokens), BF)],
        compiler_params=params(),
        cost_estimate=cost(8 * width * tokens * tokens, 2 * heads * tokens * tokens),
    )(e, qkv, stat, grad, inner)


def normed(t):
    mean = jnp.mean(t, axis=0, keepdims=True)
    centred = t - mean
    rstd = lax.rsqrt(jnp.mean(centred * centred, axis=0, keepdims=True) + NORM_EPS)
    return centred * rstd, rstd


def normed_back(grad, unit, rstd, gain):
    scaled = grad * gain
    mean = jnp.mean(scaled, axis=0, keepdims=True)
    along = jnp.mean(scaled * unit, axis=0, keepdims=True)
    return rstd * (scaled - mean - unit * along)


def gelu_and_slope(t):
    square = t * t
    inside = jnp.tanh(t * (0.7978845608028654 + (0.7978845608028654 * 0.044715) * square))
    half = 0.5 + 0.5 * inside
    slope = half + (t * (0.5 - 0.5 * inside * inside)) * (
        0.7978845608028654 + (3.0 * 0.7978845608028654 * 0.044715) * square
    )
    return t * half, slope


def lanes_sum(t):
    out = t[:, 0:128]
    for j in range(128, t.shape[1], 128):
        out = out + t[:, j : j + 128]
    return out


def column(col_ref, j):
    return col_ref[:, j : j + 1].astype(F32)


def dense_forward(signal, ctx, wo_ref, win_ref, wback_ref, col_ref, act_ref, slope_ref):
    joined = signal + dg(wo_ref[...], ctx, 0, 0) + column(col_ref, 6)
    unit_one, rstd_one = normed(joined)
    middle = unit_one * column(col_ref, 0) + column(col_ref, 1)
    low_middle = middle.astype(BF)
    width = middle.shape[0]
    summed = middle + column(col_ref, 7)
    for c in range(win_ref.shape[1] // width):
        rows = slice(c * width, (c + 1) * width)
        pre = dg(win_ref[:, rows], low_middle, 0, 0) + column(col_ref, 8 + c)
        gelu, slope = gelu_and_slope(pre)
        act = gelu.astype(BF)
        act_ref[rows, :] = act
        slope_ref[rows, :] = slope.astype(slope_ref.dtype)
        summed = summed + dg(wback_ref[:, rows], act, 1, 0)
    unit_two, rstd_two = normed(summed)
    return unit_one, rstd_one, low_middle, unit_two, rstd_two


def dense_back(grad, unit_one, rstd_one, slope_ref, unit_two, rstd_two, ctx, stat_ref, wo_ref, win_ref, wback_ref, col_ref,
               sums_ref, joined_ref, gctx_ref, inner_ref, dz_ref, du_ref, dattn_ref):
    sums_ref[2] += lanes_sum(grad * unit_two)
    sums_ref[3] += lanes_sum(grad)
    grad_summed = normed_back(grad, unit_two, rstd_two, column(col_ref, 2))
    dz = grad_summed.astype(BF)
    dz_ref[...] = dz
    sums_ref[7] += lanes_sum(dz.astype(F32))
    width = dz.shape[0]
    grad_middle = grad_summed
    for c in range(win_ref.shape[1] // width):
        rows = slice(c * width, (c + 1) * width)
        du = (dg(wback_ref[:, rows], dz, 0, 0) * slope_ref[rows, :].astype(F32)).astype(BF)
        du_ref[rows, :] = du
        sums_ref[8 + c] += lanes_sum(du.astype(F32))
        grad_middle = grad_middle + dg(win_ref[:, rows], du, 1, 0)
    sums_ref[0] += lanes_sum(grad_middle * unit_one)
    sums_ref[1] += lanes_sum(grad_middle)
    grad_joined = normed_back(grad_middle, unit_one, rstd_one, column(col_ref, 0))
    joined_ref[...] = grad_joined
    dattn = grad_joined.astype(BF)
    dattn_ref[...] = dattn
    sums_ref[6] += lanes_sum(dattn.astype(F32))
    grad_ctx = dg(wo_ref[...], dattn, 1, 0)
    for h in range(stat_ref.shape[0]):
        rows = slice(h * HEAD_DIM, (h + 1) * HEAD_DIM)
        part = (grad_ctx[rows] * stat_ref[h, 0:1, :]).astype(BF)
        gctx_ref[rows, :] = part
        inner_ref[h] = jnp.sum(part.astype(F32) * ctx[rows].astype(F32), axis=0, keepdims=True)


def tile(rows):
    return pl.BlockSpec((rows, TILE), lambda i: (0, i))


def heads_tile(heads, rows):
    return pl.BlockSpec((heads, rows, TILE), lambda i: (0, 0, i))


def rest_specs(width, hidden):
    return [
        pl.BlockSpec((width, width), lambda i: (0, 2 * hidden // width)),
        pl.BlockSpec((width, hidden), lambda i: (0, 0)),
        pl.BlockSpec((width, hidden), lambda i: (0, 1)),
    ]


def column_spec(width):
    return pl.BlockSpec((width, LANES), lambda i: (0, 3 * width // LANES))


def first_dense_kernel(signal_ref, ctx_ref, wo_ref, win_ref, wback_ref, col_ref,
                       unit_one_ref, unit_two_ref, rstd_ref, low_out_ref, act_ref, slope_ref):
    unit_one, rstd_one, _, unit_two, rstd_two = dense_forward(
        signal_ref[...].astype(F32), ctx_ref[...], wo_ref, win_ref, wback_ref, col_ref, act_ref, slope_ref)
    unit_one_ref[...] = unit_one
    unit_two_ref[...] = unit_two
    rstd_ref[0:1, :] = rstd_one
    rstd_ref[1:2, :] = rstd_two
    low_out_ref[...] = (unit_two * column(col_ref, 2) + column(col_ref, 3)).astype(BF)


def first_dense(signal, ctx, w_rest, w_first):
    width, tokens = signal.shape
    hidden = (w_rest.shape[1] - width) // 2
    return pl.pallas_call(
        first_dense_kernel,
        name="first_dense",
        grid=(tokens // TILE,),
        in_specs=[tile(width), tile(width), *rest_specs(width, hidden), column_spec(width)],
        out_specs=[tile(width), tile(width), tile(8), tile(width), tile(hidden), tile(hidden)],
        out_shape=[
            jax.ShapeDtypeStruct((width, tokens), F32),
            jax.ShapeDtypeStruct((width, tokens), F32),
            jax.ShapeDtypeStruct((8, tokens), F32),
            jax.ShapeDtypeStruct((width, tokens), BF),
            jax.ShapeDtypeStruct((hidden, tokens), BF),
            jax.ShapeDtypeStruct((hidden, tokens), BF),
        ],
        compiler_params=params(),
        cost_estimate=cost(2 * tokens * width * (width + 2 * hidden), 24 << 20, tokens * hidden),
    )(signal, ctx, w_rest, w_rest, w_rest, w_first)


def second_dense_kernel(unit_ref, ctx_ref, cot_ref, stat_ref, wo_ref, win_ref, wback_ref, col_ref,
                        out_ref, sums_ref, joined_ref, gctx_ref, inner_ref, mid_ref, act_ref, dz_ref, du_ref, dattn_ref, slope_ref):
    @pl.when(pl.program_id(0) == 0)
    def _():
        sums_ref[...] = jnp.zeros(sums_ref.shape, F32)

    ctx = ctx_ref[...]
    gain, shift = column(col_ref, 2), column(col_ref, 3)
    unit_one, rstd_one, low_middle, unit_two, rstd_two = dense_forward(
        unit_ref[...] * gain + shift, ctx, wo_ref, win_ref, wback_ref, col_ref, act_ref, slope_ref)
    mid_ref[...] = low_middle
    out_ref[...] = (unit_two * gain + shift).astype(BF).T
    dense_back(cot_ref[...].astype(F32), unit_one, rstd_one, slope_ref, unit_two, rstd_two, ctx, stat_ref,
               wo_ref, win_ref, wback_ref, col_ref, sums_ref, joined_ref, gctx_ref, inner_ref, dz_ref, du_ref, dattn_ref)


def second_dense(unit, ctx, cot, stat, w_rest, w_first):
    width, tokens = unit.shape
    hidden = (w_rest.shape[1] - width) // 2
    heads = stat.shape[0]
    return pl.pallas_call(
        second_dense_kernel,
        name="second_dense",
        grid=(tokens // TILE,),
        in_specs=[tile(width), tile(width), tile(width), heads_tile(heads, 2), *rest_specs(width, hidden), column_spec(width)],
        out_specs=[pl.BlockSpec((TILE, width), lambda i: (i, 0)), whole((12, width, LANES)), tile(width), tile(width), heads_tile(heads, 1),
                   tile(width), tile(hidden), tile(width), tile(hidden), tile(width)],
        out_shape=[
            jax.ShapeDtypeStruct((tokens, width), BF),
            jax.ShapeDtypeStruct((12, width, LANES), F32),
            jax.ShapeDtypeStruct((width, tokens), F32),
            jax.ShapeDtypeStruct((width, tokens), BF),
            jax.ShapeDtypeStruct((heads, 1, tokens), F32),
            jax.ShapeDtypeStruct((width, tokens), BF),
            jax.ShapeDtypeStruct((hidden, tokens), BF),
            jax.ShapeDtypeStruct((width, tokens), BF),
            jax.ShapeDtypeStruct((hidden, tokens), BF),
            jax.ShapeDtypeStruct((width, tokens), BF),
        ],
        scratch_shapes=[pltpu.VMEM((hidden, TILE), F32)],
        compiler_params=params(),
        cost_estimate=cost(4 * tokens * width * (width + 2 * hidden), 28 << 20, tokens * hidden),
    )(unit, ctx, cot, stat, w_rest, w_rest, w_rest, w_first)


def first_back_kernel(prior_ref, dqkv_ref, unit_one_ref, unit_two_ref, rstd_ref, slope_ref, ctx_ref, stat_ref, sums_in_ref,
                      wqkv_ref, wo_ref, win_ref, wback_ref, col_ref,
                      vec_ref, joined_ref, gctx_ref, inner_ref, mid_ref, dz_ref, du_ref, dattn_ref, sums_ref):
    step = pl.program_id(0)

    @pl.when(step == 0)
    def _():
        sums_ref[...] = sums_in_ref[...]

    unit_one = unit_one_ref[...]
    mid_ref[...] = (unit_one * column(col_ref, 0) + column(col_ref, 1)).astype(BF)
    grad = prior_ref[...] + dg(wqkv_ref[...], dqkv_ref[...], 1, 0)
    dense_back(grad, unit_one, rstd_ref[0:1, :], slope_ref, unit_two_ref[...], rstd_ref[1:2, :], ctx_ref[...], stat_ref,
               wo_ref, win_ref, wback_ref, col_ref, sums_ref, joined_ref, gctx_ref, inner_ref, dz_ref, du_ref, dattn_ref)

    @pl.when(step == pl.num_programs(0) - 1)
    def _():
        lane = lax.broadcasted_iota(jnp.int32, vec_ref.shape, 1)
        out = jnp.zeros(vec_ref.shape, F32)
        for j in (0, 1, 2, 3, 6, 7, 8, 9, 10, 11):
            out = jnp.where(lane == j, jnp.sum(sums_ref[j], axis=1, keepdims=True), out)
        vec_ref[...] = out


def first_back(prior, dqkv, unit_one, unit_two, rstd, slope, ctx, stat, sums, w_first, w_rest):
    width, tokens = prior.shape
    hidden = (w_rest.shape[1] - width) // 2
    heads = stat.shape[0]
    return pl.pallas_call(
        first_back_kernel,
        name="first_back",
        grid=(tokens // TILE,),
        in_specs=[tile(width), tile(3 * width), tile(width), tile(width), tile(8), tile(hidden), tile(width), heads_tile(heads, 2), whole(sums.shape),
                  pl.BlockSpec((width, 3 * width), lambda i: (0, 0)), *rest_specs(width, hidden), column_spec(width)],
        out_specs=[whole((width, LANES)), tile(width), tile(width), heads_tile(heads, 1), tile(width), tile(width), tile(hidden), tile(width)],
        out_shape=[
            jax.ShapeDtypeStruct((width, LANES), F32),
            jax.ShapeDtypeStruct((width, tokens), F32),
            jax.ShapeDtypeStruct((width, tokens), BF),
            jax.ShapeDtypeStruct((heads, 1, tokens), F32),
            jax.ShapeDtypeStruct((width, tokens), BF),
            jax.ShapeDtypeStruct((width, tokens), BF),
            jax.ShapeDtypeStruct((hidden, tokens), BF),
            jax.ShapeDtypeStruct((width, tokens), BF),
        ],
        scratch_shapes=[pltpu.VMEM((12, width, LANES), F32)],
        compiler_params=params(),
        cost_estimate=cost(2 * tokens * width * (4 * width + 2 * hidden), 28 << 20),
    )(prior, dqkv, unit_one, unit_two, rstd, slope, ctx, stat, sums, w_first, w_rest, w_rest, w_rest, w_first)


class Layout:
    def __init__(self, mesh_batch, mesh_shard, width):
        self.batch = mesh_batch
        self.shards = mesh_shard
        self.parts = min(mesh_batch, width // mesh_shard // 16)
        self.planes = self.parts // 2
        self.rows = width // mesh_shard // self.parts

    def swap(self, value, axis, distance):
        size = self.batch if axis == "batch" else self.shards
        return lax.ppermute(value, axis, [(i, i ^ distance) for i in range(size)])

    def place(self):
        return jnp.stack([lax.axis_index("batch") % self.parts, lax.axis_index("shard")]).astype(jnp.int32)

    def row_of(self, place_ref, c, e, d):
        block = (place_ref[1] ^ d) * self.parts + (place_ref[0] ^ (2 * e + c))
        return pl.multiple_of(block * self.rows, self.rows)

    def gather(self, mine):
        stack = jnp.concatenate([mine] + [self.swap(mine, "shard", d) for d in range(1, self.shards)], axis=0)
        plane = [stack] + [self.swap(stack, "batch", 2 * e) for e in range(1, self.planes)]
        return plane + [self.swap(s, "batch", 1) for s in plane]

    def reduce(self, keep, send):
        half = add(keep, self.swap(send, "batch", 1))
        rows = half.shape[0] // self.planes
        parts = [half[e * rows : (e + 1) * rows] for e in range(self.planes)]
        whole_plane = add(parts[0], *[self.swap(parts[e], "batch", 2 * e) for e in range(1, self.planes)])
        blocks = [whole_plane[d * self.rows : (d + 1) * self.rows] for d in range(self.shards)]
        own = add(blocks[0], *[self.swap(blocks[d], "shard", d) for d in range(1, self.shards)])
        distance = self.parts
        while distance < self.batch:
            own = add(own, self.swap(own, "batch", distance))
            distance *= 2
        return own

    def total(self, own):
        own = tree([own] + [self.swap(own, "shard", d) for d in range(1, self.shards)])
        own = tree([own] + [self.swap(own, "batch", 2 * e) for e in range(1, self.planes)])
        return own + self.swap(own, "batch", 1)

    def spread(self, own):
        plane = [own] + [self.swap(own, "batch", 2 * e) for e in range(1, self.planes)]
        other = [self.swap(s, "batch", 1) for s in plane]
        return jnp.concatenate([t for pair in zip(plane, other, strict=True) for t in pair], axis=0)


def tree(values):
    while len(values) > 1:
        values = [a + b for a, b in zip(values[::2], values[1::2], strict=True)]
    return values[0]


def add(first, *others):
    total = first.astype(F32)
    for other in others:
        total = total + other.astype(F32)
    return total.astype(BF)


def collect_kernel(layout, place_ref, *refs):
    sources, out_ref, sem = refs[:-2], refs[-2], refs[-1]
    copies = []
    for c in range(2):
        for e in range(layout.planes):
            for d in range(layout.shards):
                copies.append(pltpu.make_async_copy(
                    sources[c * layout.planes + e].at[pl.ds(d * layout.rows, layout.rows)],
                    out_ref.at[pl.ds(layout.row_of(place_ref, c, e, d), layout.rows)],
                    sem.at[len(copies)],
                ))
    for copy in copies:
        copy.start()
    for copy in copies:
        copy.wait()


def collect(layout, place, sources):
    rows = layout.rows * layout.parts * layout.shards
    columns = sources[0].shape[1]
    return pl.pallas_call(
        functools.partial(collect_kernel, layout),
        name="collect",
        in_specs=[pl.BlockSpec(memory_space=pltpu.SMEM)] + [pl.BlockSpec(memory_space=pl.ANY)] * len(sources),
        out_specs=pl.BlockSpec(memory_space=pl.ANY),
        out_shape=jax.ShapeDtypeStruct((rows, columns), BF),
        scratch_shapes=[pltpu.SemaphoreType.DMA((layout.parts * layout.shards,))],
        compiler_params=params(),
        cost_estimate=cost(0, 4 * rows * columns),
    )(place, *sources)


def in_order(layout, place_ref, source_ref, target_ref):
    at = 0
    for c in range(2):
        for e in range(layout.planes):
            for d in range(layout.shards):
                target_ref[at : at + layout.rows] = source_ref[pl.ds(layout.row_of(place_ref, c, e, d), layout.rows), :]
                at += layout.rows


def weight_kernel(layout, place_ref, la_ref, lb_ref, ra_ref, rb_ref, keep_ref, send_ref, left_ref):
    @pl.when(pl.program_id(0) == 0)
    def _():
        in_order(layout, place_ref, la_ref, left_ref.at[0])
        in_order(layout, place_ref, lb_ref, left_ref.at[1])

    out = (dg(left_ref[0], ra_ref[...], 1, 1) + dg(left_ref[1], rb_ref[...], 1, 1)).astype(BF)
    half = out.shape[0] // 2
    keep_ref[...] = out[:half]
    send_ref[...] = out[half:]


def weight_grad(layout, place, left_one, left_two, right_one, right_two, block):
    rows, tokens = left_one.shape
    columns = right_one.shape[0]
    half = jax.ShapeDtypeStruct((rows // 2, columns), BF)
    return pl.pallas_call(
        functools.partial(weight_kernel, layout),
        name="weight_grad",
        grid=(columns // block,),
        in_specs=[pl.BlockSpec(memory_space=pltpu.SMEM), whole((rows, tokens)), whole((rows, tokens)),
                  pl.BlockSpec((block, tokens), lambda i: (i, 0)), pl.BlockSpec((block, tokens), lambda i: (i, 0))],
        out_specs=[pl.BlockSpec((rows // 2, block), lambda i: (0, i))] * 2,
        out_shape=[half, half],
        scratch_shapes=[pltpu.VMEM((2, rows, tokens), BF)],
        compiler_params=params(),
        cost_estimate=cost(4 * rows * columns * tokens, 4 * (rows + columns) * tokens + 2 * rows * columns),
    )(place, left_one, left_two, right_one, right_two)


def last_back_kernel(layout, first_pair, place_ref, e_ref, qkv_ref, stat_ref, grad_ref, inner_ref, act_one_ref, act_two_ref, dqkv_two_ref, vec_in_ref,
                     out_ref, keep_ref, send_ref, vec_ref, vec_keep_ref, vec_send_ref, ds_ref, left_ref, order_ref):
    step = pl.program_id(0)

    @pl.when(step == 0)
    def _():
        in_order(layout, place_ref, act_one_ref, left_ref.at[0])
        in_order(layout, place_ref, act_two_ref, left_ref.at[1])
        vec_ref[...] = vec_in_ref[...]

    attend_back_kernel(e_ref, qkv_ref, stat_ref, grad_ref, inner_ref, out_ref, ds_ref)
    pair = out_ref.shape[1]
    for t in range(3):
        total = (dg(left_ref[0], out_ref[t], 1, 1) + dg(left_ref[1], dqkv_two_ref[t], 1, 1)).astype(BF)
        half = total.shape[0] // 2
        keep_ref[:, t * pair : (t + 1) * pair] = total[:half]
        send_ref[:, t * pair : (t + 1) * pair] = total[half:]
    rows = pl.ds(pl.multiple_of((first_pair + step) * pair, pair), pair)
    lane = lax.broadcasted_iota(jnp.int32, (pair, LANES), 1)
    vec = vec_ref[rows, :]
    for lane_at, t in ((4, 0), (5, 2)):
        both = lanes_sum(out_ref[t].astype(F32)) + lanes_sum(dqkv_two_ref[t].astype(F32))
        vec = jnp.where(lane == lane_at, jnp.sum(both, axis=1, keepdims=True), vec)
    vec_ref[rows, :] = vec

    @pl.when(step == pl.num_programs(0) - 1)
    def _():
        in_order(layout, place_ref, vec_ref, order_ref)
        half = order_ref.shape[0] // 2
        vec_keep_ref[...] = order_ref[0:half].astype(BF)
        vec_send_ref[...] = order_ref[half:].astype(BF)


def last_back(layout, place, first_pair, pairs, e, qkv, stat, grad, inner, act_one, act_two, dqkv_two, vec):
    heads, tokens, _ = e.shape
    width = grad.shape[0]
    pair = 2 * HEAD_DIM
    half = jax.ShapeDtypeStruct((width // 2, 3 * pair * pairs), BF)
    vec_half = jax.ShapeDtypeStruct((width // 2, LANES), BF)
    return pl.pallas_call(
        functools.partial(last_back_kernel, layout, first_pair),
        name="last_back",
        grid=(pairs,),
        in_specs=[
            pl.BlockSpec(memory_space=pltpu.SMEM),
            pl.BlockSpec((2, tokens, tokens), lambda i: (first_pair + i, 0, 0)),
            pl.BlockSpec((3, pair, tokens), lambda i: (0, first_pair + i, 0)),
            pl.BlockSpec((2, 2, tokens), lambda i: (first_pair + i, 0, 0)),
            pl.BlockSpec((pair, tokens), lambda i: (first_pair + i, 0)),
            pl.BlockSpec((2, 1, tokens), lambda i: (first_pair + i, 0, 0)),
            whole((width, tokens)),
            whole((width, tokens)),
            pl.BlockSpec((3, pair, tokens), lambda i: (0, first_pair + i, 0)),
            whole((width, LANES)),
        ],
        out_specs=[
            pl.BlockSpec((3, pair, tokens), lambda i: (0, i, 0)),
            pl.BlockSpec((width // 2, 3 * pair), lambda i: (0, i)),
            pl.BlockSpec((width // 2, 3 * pair), lambda i: (0, i)),
            whole((width, LANES)),
            whole((width // 2, LANES)),
            whole((width // 2, LANES)),
        ],
        out_shape=[
            jax.ShapeDtypeStruct((3, pair * pairs, tokens), BF),
            half,
            half,
            jax.ShapeDtypeStruct((width, LANES), F32),
            vec_half,
            vec_half,
        ],
        scratch_shapes=[pltpu.VMEM((2, tokens, tokens), BF), pltpu.VMEM((2, width, tokens), BF), pltpu.VMEM((width, LANES), F32)],
        compiler_params=params(),
        cost_estimate=cost(pairs * (16 * pair * tokens * tokens + 12 * width * pair * tokens), pairs * 4 * tokens * tokens + 4 * width * tokens),
    )(place, e, qkv, stat, grad, inner, act_one, act_two, dqkv_two, vec)


def input_kernel(joined_ref, *refs):
    pieces, w_ref, out_ref = refs[:-2], refs[-2], refs[-1]
    total = joined_ref[...]
    pair = 2 * HEAD_DIM
    width = total.shape[0]
    at = 0
    for piece in pieces:
        rows = piece.shape[1]
        for t in range(3):
            total = total + dg(w_ref[:, t * width + at : t * width + at + rows], piece[t], 1, 0)
        at += rows
    out_ref[...] = total.T


def input_gradient(joined, pieces, w_first):
    width, tokens = joined.shape
    return pl.pallas_call(
        input_kernel,
        name="input_gradient",
        grid=(tokens // TILE,),
        in_specs=[tile(width)] + [heads_tile(3, p.shape[1]) for p in pieces] + [pl.BlockSpec((width, 3 * width), lambda i: (0, 0))],
        out_specs=pl.BlockSpec((TILE, width), lambda i: (i, 0)),
        out_shape=jax.ShapeDtypeStruct((tokens, width), F32),
        compiler_params=params(),
        cost_estimate=cost(6 * width * width * tokens, 8 << 20),
    )(joined, *pieces, w_first)


def adam_kernel(pieces, place_ref, factor_ref, *refs):
    del place_ref
    grads = refs[: len(pieces)]
    w_ref, one_ref, two_ref, vec_ref, v_ref, vone_ref, vtwo_ref = refs[len(pieces) : len(pieces) + 7]
    gw_ref, nw_ref, none_ref, ntwo_ref, gv_ref, nv_ref, nvone_ref, nvtwo_ref, hold_ref = refs[len(pieces) + 7 :]
    factor = factor_ref[0]
    for grad_ref, spans in zip(grads, pieces, strict=True):
        for source, target, size in spans:
            to = slice(target, target + size)
            grad = grad_ref[:, source : source + size].astype(F32)
            gw_ref[:, to] = grad
            nw_ref[:, to], none_ref[:, to], ntwo_ref[:, to] = adam_update(w_ref[:, to], one_ref[:, to], two_ref[:, to], grad * factor)
    step = pl.program_id(0)
    rows = vec_ref.shape[0]
    hold_ref[pl.ds(pl.multiple_of(step * rows, rows), rows), :] = vec_ref[...].astype(F32)

    @pl.when(step == pl.num_programs(0) - 1)
    def _():
        grad = hold_ref[...].T[0 : gv_ref.shape[0], 0 : gv_ref.shape[1]]
        gv_ref[...] = grad
        nv_ref[...], nvone_ref[...], nvtwo_ref[...] = adam_update(v_ref[...], vone_ref[...], vtwo_ref[...], grad * factor)


def adam(layout, place, factor, pieces, grads, vec, weights, first, second, vectors, vector_first, vector_second):
    rows, columns = weights.shape
    block = layout.rows
    natural = pl.BlockSpec((block, columns), lambda i, place, factor: (i, 0))
    small = pl.BlockSpec(vectors.shape, lambda i, place, factor: (0, 0))

    def relative(width):
        return pl.BlockSpec((block, width), lambda i, place, factor: (i ^ place[0], 0))

    big = jax.ShapeDtypeStruct((rows, columns), F32)
    little = jax.ShapeDtypeStruct(vectors.shape, F32)
    return pl.pallas_call(
        functools.partial(adam_kernel, pieces),
        name="adam",
        grid_spec=pltpu.PrefetchScalarGridSpec(
            num_scalar_prefetch=2,
            grid=(rows // block,),
            in_specs=[relative(g.shape[1]) for g in grads] + [natural] * 3 + [relative(LANES)] + [small] * 3,
            out_specs=[natural] * 4 + [small] * 4,
            scratch_shapes=[pltpu.VMEM((LANES, LANES), F32)],
        ),
        out_shape=[big] * 4 + [little] * 4,
        compiler_params=params(),
        cost_estimate=cost(20 * rows * columns, 30 * rows * columns, rows * columns),
    )(place, factor, *grads, weights, first, second, vec, vectors, vector_first, vector_second)


def masks(segments, tags, length):
    tokens = segments.shape[0]
    matches = segments[None, :] == jnp.arange(tags.shape[0], dtype=jnp.int32)[:, None]
    group = jnp.sum(jnp.where(matches, tags[:, None], 0), axis=0)
    live = jnp.arange(tokens, dtype=jnp.int32) < length
    kinds = jnp.arange(16, dtype=jnp.int32)[:, None]
    same = group[None, :] == kinds
    kmask = jnp.where(kinds < 4, (same & live[None, :]).astype(F32), jnp.where(kinds == 4, (~live)[None, :].astype(F32), 0.0))
    qmask = jnp.where(kinds < 4, jnp.where(same, 0.0, -FAR), jnp.where(kinds == 4, -FAR, 0.0))
    return kmask.astype(BF), jnp.broadcast_to(qmask, (16, tokens)).astype(BF)


def squares(t):
    return jnp.sum(jnp.square(t.astype(F32)))


def on_device(layout, inputs, cotangent, lengths, segment_ids, group_tags, weights, first_moments, second_moments, vectors, vector_first, vector_second):
    _, tokens, width = inputs.shape
    hidden = (weights.shape[1] - 4 * width) // 2
    pair = 2 * HEAD_DIM
    place = layout.place()
    at = place[0] * layout.rows
    my_weights = lax.dynamic_slice_in_dim(weights, at, layout.rows, 0).astype(BF)
    my_vectors = lax.dynamic_slice_in_dim(jnp.pad(vectors.T, ((0, 0), (0, LANES - vectors.shape[0]))), at, layout.rows, 0).astype(BF)
    first_blocks = layout.gather(jnp.concatenate([my_weights[:, : 3 * width], my_vectors], axis=1))
    rest_blocks = layout.gather(jnp.concatenate([my_weights[:, 4 * width :], my_weights[:, 3 * width : 4 * width]], axis=1))
    kmask, qmask = masks(segment_ids[0], group_tags[0], lengths[0])
    act_one = inputs[0].T
    cot = cotangent[0].T

    w_first = collect(layout, place, first_blocks)
    e_one, ctx_one, qkv_one, stat_one = attend(act_one, w_first, kmask, qmask)
    w_rest = collect(layout, place, rest_blocks)
    unit_one, unit_two, rstd, act_two, hid_one, slope = first_dense(act_one, ctx_one, w_rest, w_first)
    e_two, ctx_two, qkv_two, stat_two = attend(act_two, w_first, kmask, qmask)
    outputs, sums, joined_two, gctx_two, inner_two, mid_two, hid_two, dz_two, du_two, dattn_two = second_dense(
        unit_two, ctx_two, cot, stat_two, w_rest, w_first)
    dqkv_two = attend_back(e_two, qkv_two, stat_two, gctx_two, inner_two)
    vec, joined_one, gctx_one, inner_one, mid_one, dz_one, du_one, dattn_one = first_back(
        joined_two, dqkv_two.reshape(3 * width, tokens), unit_one, unit_two, rstd, slope, ctx_one, stat_one, sums, w_first, w_rest)

    owned = []
    owned.append(layout.reduce(*weight_grad(layout, place, mid_one, mid_two, du_one, du_two, width)))
    owned.append(layout.reduce(*weight_grad(layout, place, dz_one, dz_two, hid_one, hid_two, width)))
    owned.append(layout.reduce(*weight_grad(layout, place, ctx_one, ctx_two, dattn_one, dattn_two, width)))
    spans = [[(0, 4 * width, hidden)], [(0, 4 * width + hidden, hidden)], [(0, 3 * width, width)]]
    pairs = width // pair
    group = pairs // 2
    dqkv = []
    for start in range(0, pairs, group):
        out, keep, send, vec, vec_keep, vec_send = last_back(
            layout, place, start, group, e_one, qkv_one, stat_one, gctx_one, inner_one, act_one, act_two, dqkv_two, vec)
        dqkv.append(out)
        spans.append([((i * 3 + t) * pair, t * width + (start + i) * pair, pair) for i in range(group) for t in range(3)])
        if start + group == pairs:
            keep, send = jnp.concatenate([keep, vec_keep], axis=1), jnp.concatenate([send, vec_send], axis=1)
        owned.append(layout.reduce(keep, send))
    grads = [layout.spread(t) for t in owned]
    vec_grad = grads[-1][:, 3 * pair * group :]
    grad_norm = jnp.sqrt(layout.total(sum(squares(t) for t in owned)))
    input_grad = input_gradient(joined_one, dqkv, w_first)
    clip_limit = math.sqrt(width * weights.shape[1])
    factor = clip_limit / jnp.maximum(grad_norm, clip_limit)
    updated = adam(layout, place, factor.reshape(1), spans, grads, vec_grad, weights, first_moments, second_moments, vectors, vector_first, vector_second)
    grad_w, new_weights, new_first, new_second, grad_v, new_vectors, new_vector_first, new_vector_second = updated
    return (
        outputs[None],
        input_grad[None],
        grad_w,
        grad_v,
        grad_norm,
        new_weights,
        new_first,
        new_second,
        new_vectors,
        new_vector_first,
        new_vector_second,
    )


def solution(mesh):
    rows = ("batch", "shard")
    placed = (
        P(rows, None, None),
        P(rows, None, None),
        P(rows),
        P(rows, None),
        P(rows, None),
        P("shard", None),
        P("shard", None),
        P("shard", None),
        P(None, "shard"),
        P(None, "shard"),
        P(None, "shard"),
    )
    return jax.shard_map(
        functools.partial(on_device, Layout(mesh.shape["batch"], mesh.shape["shard"], D)),
        mesh=mesh,
        in_specs=placed,
        out_specs=(
            P(rows, None, None),
            P(rows, None, None),
            P("shard", None),
            P(None, "shard"),
            P(),
            P("shard", None),
            P("shard", None),
            P("shard", None),
            P(None, "shard"),
            P(None, "shard"),
            P(None, "shard"),
        ),
        check_vma=False,
    )
```

time: 564 us -> 635 us (1.13)
  Pallas kernels: 185 us -> 399 us
  waiting for transfers between devices: 271 us -> 110 us
  starting transfers between devices: 0.16 us -> 91.9 us
  blocking collectives: 39.3 us -> 0 us
  other arithmetic: 22.4 us -> 6.24 us
  local copies, waits for them, and re-layouts: 18.6 us -> 7.4 us
  between operations: 18.3 us -> 11.4 us
    pallas_call x4 -> x8, Pallas kernels: 32.7 us -> 269 us  [the longest x2 199 us: collect(): pl.pallas_call(functools.partial(collect_kernel, layout), name='collect',...]
    ppermute x0 -> x97, waiting for transfers between devices: none -> 110 us  [swap(): return lax.ppermute(value, axis, [(i, i ^ distance) for i in range(size)])]
    reduce_scatter x1 -> x0, waiting for transfers between devices: 105 us -> none  [on_device(): lax.psum_scatter(weight_grads, 'shard', scatter_dimension=0, tiled=True)]
    all_gather x1 -> x0, waiting for transfers between devices: 96.1 us -> none  [on_device(): matrices = lax.all_gather(weights.astype(BF), 'shard', axis=0, tiled=True)]
    ppermute x0 -> x97, starting transfers between devices: none -> 91.9 us  [swap(): return lax.ppermute(value, axis, [(i, i ^ distance) for i in range(size)])]
    psum x1 -> x0, waiting for transfers between devices: 47.3 us -> none  [on_device(): own_weight = lax.psum(own_weight, 'batch').astype(F32)]
    psum x2 -> x0, blocking collectives: 24.2 us -> none  [the longest x1 12.3 us: on_device(): lax.psum(jnp.sum(own_weight * own_weight) + jnp.sum(own_vector * own_vect...]
    unnamed x5 -> x0, waiting for transfers between devices: 22.6 us -> none
  transfers between devices with their start and end apart: 4 -> 97, of which waited for: 4 -> 49; matrix products, arithmetic and copies ran while one was open for 2% -> 2% of each run, Pallas kernels for 0% -> 22%
where the time goes in v2:
time: 635 us; the launch traced here: 626 us
  Pallas kernels  399 us (63%)
  waiting for transfers between devices  110 us (17%)
  starting transfers between devices  91.9 us (14%)
  between operations  11.4 us (2%)
  local copies, waits for them, and re-layouts  7.4 us (1%)
    pallas_call x2, Pallas kernels, collect(): pl.pallas_call(functools.partial(collect_kernel, layout), name='collect',...  199 us
    ppermute x97, waiting for transfers between devices, swap(): return lax.ppermute(value, axis, [(i, i ^ distance) for i in range(size)])  110 us
    ppermute x97, starting transfers between devices, swap(): return lax.ppermute(value, axis, [(i, i ^ distance) for i in range(size)])  91.9 us
    pallas_call x2, Pallas kernels, attend(): pl.pallas_call(attend_kernel, name='attend', grid=(pairs,), in_specs=[who...  36.5 us
    pallas_call x2, Pallas kernels, last_back(): pl.pallas_call(functools.partial(last_back_kernel, layout, first_pair), n...  35.8 us
    pallas_call x1, Pallas kernels, second_dense(): pl.pallas_call(second_dense_kernel, name='second_dense', grid=(tokens //...  26.6 us
    pallas_call x1, Pallas kernels, first_back(): pl.pallas_call(first_back_kernel, name='first_back', grid=(tokens // TILE...  23 us
    pallas_call x3, Pallas kernels, weight_grad(): pl.pallas_call(functools.partial(weight_kernel, layout), name='weight_gra...  21.7 us
  transfers between devices with their start and end apart: 97, of which 49 were waited for; matrix products, arithmetic and copies ran while one was open for 2% of the time, Pallas kernels for 22%

profile of v2, /device:TPU:0, one launch (start us, length us, event | category | flops | bytes accessed | tf_op | source)
XLA Modules:
  0.0 625.9 jit_solution(14746273137316465851)
XLA Ops:
  2.7 5.1 collective-permute-start.2
  8.5 3.8 collective-permute-start.12
  12.9 5.4 collective-permute-done.1
  18.4 6.8 %collective-permute-done.11 = bf16[16,4608]{1,0:T(8,128)(2,1)S(1)} collective-permute-done((bf16[16,4608]{1,0:T(8,128)(2,1)S(1)}, bf16[16,4608]{1,0:T(8,128)(2,1)S(1)}, u32[]{:S(2)}, u32[]{:S(2)}) %collective-permute-start.11) | collective-permute-done | bytes 147488 | tf_op jit(solution)/shard_map/ppermute | solution.py:438
  25.2 2.5 collective-permute-start.15
  28.8 2.4 collective-permute-start.5
  32.6 25.5 %collective-permute-done.5.refs_3_ = bf16[64,1664]{1,0:T(8,128)(2,1)} collective-permute-done((bf16[64,1664]{1,0:T(8,128)(2,1)S(1)}, bf16[64,1664]{1,0:T(8,128)(2,1)}, u32[]{:S(2)}, u32[]{:S(2)}) %collective-permute-start.5) | collective-permute-done | bytes 213024 | tf_op jit(solution)/shard_map/ppermute | solution.py:438
  59.6 2.9 collective-permute-done.4.refs_2_
  71.0 53.7 %collect.2.wq_ref.wk_ref.wv_ref.col_ref.wqkv_ref.refs_2_ = bf16[512,1664]{1,0:T(8,128)(2,1)} custom-call(s32[2]{0:T(128)} %pad_add_fusion.place_ref, bf16[64,1664]{1,0:T(8,128)(2,1)} %copy-done.5, bf16[64,1664]{1,0:T(8,128)(2,1)} %copy-done.15, bf16[64,1664]{1,0:T(8,128)(2,1)} %collective-permute-done.4.refs_2_, ...), custom_call_target="tpu_custom_call" | custom-call | bytes 3407872 | tf_op jit(solution)/shard_map/collect/pallas_call | solution.py:509
  124.6 21.1 %attend.2 = (bf16[8,1024,1024]{2,1,0:T(8,128)(2,1)}, bf16[512,1024]{1,0:T(8,128)(2,1)}, bf16[3,512,1024]{2,1,0:T(8,128)(2,1)}, f32[8,2,1024]{2,1,0:T(2,128)}) custom-call(bf16[512,1024]{1,0:T(8,128)(2,1)} %bitcast.18, bf16[512,1664]{1,0:T(8,128)(2,1)} %collect.2.wq_ref.wk_ref.wv_ref.col_ref.wqkv_ref.refs_2_, ...), custom_call_target="tpu_custom_call" | custom-call | flops 3758096384 | bytes 16777216 | tf_op jit(solution)/shard_map/attend/pallas_call | solution.py:123
  145.8 145.0 %collect.3.wo_ref.win_ref.wback_ref = bf16[512,4608]{1,0:T(8,128)(2,1)} custom-call(s32[2]{0:T(128)} %pad_add_fusion.place_ref, bf16[64,4608]{1,0:T(8,128)(2,1)} %copy-done, bf16[64,4608]{1,0:T(8,128)(2,1)} %collective-permute-done.13.refs_1_, bf16[64,4608]{1,0:T(8,128)(2,1)} %collective-permute-done.14.refs_2_, bf16[64,4608]{1,0:T(8,128)(2,1)} %copy-done.8, ...), custom_call_target="tpu_custom_call" | custom-call | bytes 9437184 | tf_op jit(solution)/shard_map/collect/pallas_call | solution.py:509
  290.8 15.9 %first_dense.1 = (f32[512,1024]{1,0:T(8,128)}, f32[512,1024]{1,0:T(8,128)}, f32[8,1024]{1,0:T(8,128)}, bf16[512,1024]{1,0:T(8,128)(2,1)}, bf16[2048,1024]{1,0:T(8,128)(2,1)}, /*index=5*/bf16[2048,1024]{1,0:T(8,128)(2,1)}) custom-call(bf16[512,1024]{1,0:T(8,128)(2,1)} %bitcast.19, bf16[512,1024]{1,0:T(8,128)(2,1)} %get-tuple-element.66.ctx_ref.la_ref, ...), custom_call_target="tpu_custom_call" | custom-call | flops 4831838208 | bytes 25165824 | tf_op jit(solution)/shard_map/first_dense/pallas_call | solution.py:313
  306.7 15.4 %attend.3 = (bf16[8,1024,1024]{2,1,0:T(8,128)(2,1)}, bf16[512,1024]{1,0:T(8,128)(2,1)}, bf16[3,512,1024]{2,1,0:T(8,128)(2,1)}, f32[8,2,1024]{2,1,0:T(2,128)}) custom-call(bf16[512,1024]{1,0:T(8,128)(2,1)} %get-tuple-element.68.act_ref.act_two_ref, bf16[512,1664]{1,0:T(8,128)(2,1)} %collect.2.wq_ref.wk_ref.wv_ref.col_ref.wqkv_ref.refs_2_, ...), custom_call_target="tpu_custom_call" | custom-call | flops 3758096384 | bytes 16777216 | tf_op jit(solution)/shard_map/attend/pallas_call | solution.py:123
  322.1 26.6 %second_dense.1 = (bf16[1024,512]{1,0:T(8,128)(2,1)}, f32[12,512,128]{2,1,0:T(8,128)}, f32[512,1024]{1,0:T(8,128)}, bf16[512,1024]{1,0:T(8,128)(2,1)}, f32[8,1,1...) custom-call(f32[512,1024]{1,0:T(8,128)} %get-tuple-element.67.unit_r, ...), custom_call_target="tpu_custom_call" | custom-call | flops 9663676416 | bytes 29360128 | tf_op jit(solution)/shard_map/second_dense/pallas_call | solution.py:352
  348.6 21.5 %attend_back.1.dqkv_two_ref = bf16[3,512,1024]{2,1,0:T(8,128)(2,1)} custom-call(bf16[8,1024,1024]{2,1,0:T(8,128)(2,1)} %get-tuple-element.73.e_ref, bf16[3,512,1024]{2,1,0:T(8,128)(2,1)} %get-tuple-element.74.qkv_ref, f32[8,2,1024]{2,1,0:T(2,128)} %get-tuple-element.70.stat_ref, bf16[512,1024]{1,0:T(8,128)(2,1)} %get-tuple-element.75.grad_ref, ...), custom_call_target="tpu_custom_call" | custom-call | flops 4294967296 | bytes 16777216 | tf_op jit(solution)/shard_map/attend_back/pallas_call | solution.py:175
  370.1 23.0 %first_back.1 = (f32[512,128]{1,0:T(8,128)}, f32[512,1024]{1,0:T(8,128)}, bf16[512,1024]{1,0:T(8,128)(2,1)}, f32[8,1,1024]{2,1,0:T(1,128)}, bf16[512,1024]{1,0:T...) custom-call(f32[512,1024]{1,0:T(8,128)} %get-tuple-element.72.prior_ref, ...), custom_call_target="tpu_custom_call" | custom-call | flops 6442450944 | bytes 29360128 | tf_op jit(solution)/shard_map/first_back/pallas_call | solution.py:405
  393.1 4.2 weight_grad.5
  397.7 8.8 %weight_grad.3 = (bf16[256,2048]{1,0:T(8,128)(2,1)}, bf16[256,2048]{1,0:T(8,128)(2,1)}) custom-call(s32[2]{0:T(128)} %pad_add_fusion.place_ref, bf16[512,1024]{1,0:T(8,128)(2,1)} %get-tuple-element.91.la_ref, bf16[512,1024]{1,0:T(8,128)(2,1)} %get-tuple-element.92.lb_ref, bf16[2048,1024]{1,0:T(8,128)(2,1)} %get-tuple-element.93.ra_ref, ...), custom_call_target="tpu_custom_call" | custom-call | flops 4294967296 | bytes 12582912 | tf_op jit(solution)/shard_map/weight_grad/pallas_call | solution.py:546
  406.6 17.9 %last_back.2 = (bf16[3,256,1024]{2,1,0:T(8,128)(2,1)}, bf16[256,768]{1,0:T(8,128)(2,1)}, bf16[256,768]{1,0:T(8,128)(2,1)}, f32[512,128]{1,0:T(8,128)}, bf16[256,...) custom-call(s32[2]{0:T(128)} %pad_add_fusion.place_ref, bf16[8,1024,1024]{2,1,0:T(8,128)(2,1)} %get-tuple-element.83.e_ref, ...), custom_call_target="tpu_custom_call" | custom-call | flops 5905580032 | bytes 10485760 | tf_op jit(solution)/shard_map/last_back/pallas_call | solution.py:599
  424.5 17.8 %last_back.3 = (bf16[3,256,1024]{2,1,0:T(8,128)(2,1)}, bf16[256,768]{1,0:T(8,128)(2,1)}, bf16[256,768]{1,0:T(8,128)(2,1)}, f32[512,128]{1,0:T(8,128)}, bf16[256,...) custom-call(s32[2]{0:T(128)} %pad_add_fusion.place_ref, bf16[8,1024,1024]{2,1,0:T(8,128)(2,1)} %get-tuple-element.83.e_ref, ...), custom_call_target="tpu_custom_call" | custom-call | flops 5905580032 | bytes 10485760 | tf_op jit(solution)/shard_map/last_back/pallas_call | solution.py:599
  442.8 8.8 %weight_grad.4 = (bf16[256,2048]{1,0:T(8,128)(2,1)}, bf16[256,2048]{1,0:T(8,128)(2,1)}) custom-call(s32[2]{0:T(128)} %pad_add_fusion.place_ref, bf16[512,1024]{1,0:T(8,128)(2,1)} %get-tuple-element.97.la_ref, bf16[512,1024]{1,0:T(8,128)(2,1)} %get-tuple-element.98.lb_ref, bf16[2048,1024]{1,0:T(8,128)(2,1)} %get-tuple-element.99.ra_ref, ...), custom_call_target="tpu_custom_call" | custom-call | flops 4294967296 | bytes 12582912 | tf_op jit(solution)/shard_map/weight_grad/pallas_call | solution.py:546
  455.2 6.6 %input_gradient.1 = f32[1024,512]{1,0:T(8,128)} custom-call(f32[512,1024]{1,0:T(8,128)} %get-tuple-element.82.joined_ref, bf16[3,256,1024]{2,1,0:T(8,128)(2,1)} %get-tuple-element.88.refs_0_, bf16[3,256,1024]{2,1,0:T(8,128)(2,1)} %get-tuple-element.90.refs_1_, bf16[512,1664]{1,0:T(8,128)(2,1)} %collect.2.wq_ref.wk_ref.wv_ref.col_ref.wqkv_ref.refs_2_), custom_call_target="tpu_custom_call" | custom-call | flops 1610612736 | bytes 8388608 | tf_op jit(solution)/shard_map/input_gradient/pallas_call | solution.py:653
  462.1 2.9 collective-permute-start.40
  465.8 1.9 collective-permute-done.40
  467.7 2.0 collective-permute-done.39
  483.9 3.2 collective-permute-done.44
  497.9 1.7 collective-permute-done.84
  500.3 3.2 collective-permute-done.86
  504.9 3.3 collective-permute-done.88
  508.8 4.2 collective-permute-done.50
  517.0 2.9 collective-permute-done.54
  520.4 1.7 collective-permute-start.95
  536.4 2.8 collective-permute-done.21
  540.1 5.1 collective-permute-done.23
  545.2 1.9 collective-permute-done.22
  548.1 1.8 collective-permute-start.26
  551.5 4.2 collective-permute-done.30
  558.1 1.8 collective-permute-start.33
  570.3 1.7 collective-permute-start.55
  572.0 1.8 collective-permute-done.55
  573.8 3.2 collective-permute-start.57
  580.6 3.1 collective-permute-done.56
  584.9 2.4 collective-permute-start.58
  588.5 2.9 collective-permute-start.60
  593.0 2.8 collective-permute-start.59
  599.1 1.6 collective-permute-start.74
  604.6 3.3 collective-permute-done.70
  611.4 12.9 %adam.1 = (f32[128,6144]{1,0:T(8,128)}, f32[128,6144]{1,0:T(8,128)}, f32[128,6144]{1,0:T(8,128)}, f32[128,6144]{1,0:T(8,128)}, f32[12,128]{1,0:T(8,128)}, /*inde...) custom-call(s32[2]{0:T(128)} %pad_add_fusion.place_ref, f32[1]{0:T(128)} %bitcast.14.factor_ref, ...), custom_call_target="tpu_custom_call" | custom-call | flops 15728640 | bytes 23592960 | tf_op jit(solution)/shard_map/adam/pallas_call | solution.py:699
  (296 shorter events, 93.6 us)
Async XLA Ops:
  2.7 9.6 %collective-permute-start.2 = (bf16[16,1664]{1,0:T(8,128)(2,1)S(1)}, bf16[16,1664]{1,0:T(8,128)(2,1)S(1)}, u32[]{:S(2)}, u32[]{:S(2)}) collective-permute-start(bf16[16,1664]{1,0:T(8,128)(2,1)S(1)} %pad_maximum_fusion.4), channel_id=1, source_target_pairs={{0,3},{1,2},{2,1},{3,0},{4,7},{5,6},{6,5},{7,4},{8,11},{9,10},{10,... | collective-permute-start | bytes 159752 | tf_op jit(solution)/shard_map/ppermute | solution.py:438
  7.8 10.5 %collective-permute-start.1 = (bf16[16,1664]{1,0:T(8,128)(2,1)S(1)}, bf16[16,1664]{1,0:T(8,128)(2,1)S(1)}, u32[]{:S(2)}, u32[]{:S(2)}) collective-permute-start(bf16[16,1664]{1,0:T(8,128)(2,1)S(1)} %pad_maximum_fusion.4), channel_id=1, source_target_pairs={{0,2},{1,3},{2,0},{3,1},{4,6},{5,7},{6,4},{7,5},{8,10},{9,11},{10,... | collective-permute-start | bytes 159752 | tf_op jit(solution)/shard_map/ppermute | solution.py:438
  7.8 10.5 %collective-permute-start = (bf16[16,1664]{1,0:T(8,128)(2,1)S(1)}, bf16[16,1664]{1,0:T(8,128)(2,1)S(1)}, u32[]{:S(2)}, u32[]{:S(2)}) collective-permute-start(bf16[16,1664]{1,0:T(8,128)(2,1)S(1)} %pad_maximum_fusion.4), channel_id=1, source_target_pairs={{0,1},{1,0},{2,3},{3,2},{4,5},{5,4},{6,7},{7,6},{8,9},{9,8},{10,11... | collective-permute-start | bytes 159752 | tf_op jit(solution)/shard_map/ppermute | solution.py:438
  8.5 9.9 %collective-permute-start.12 = (bf16[16,4608]{1,0:T(8,128)(2,1)S(1)}, bf16[16,4608]{1,0:T(8,128)(2,1)S(1)}, u32[]{:S(2)}, u32[]{:S(2)}) collective-permute-start(bf16[16,4608]{1,0:T(8,128)(2,1)S(1)} %pad_maximum_fusion.3), channel_id=1, source_target_pairs={{0,3},{1,2},{2,1},{3,0},{4,7},{5,6},{6,5},{7,4},{8,11},{9,10},{10,... | collective-permute-start | bytes 442376 | tf_op jit(solution)/shard_map/ppermute | solution.py:438
  12.3 12.9 %collective-permute-start.11 = (bf16[16,4608]{1,0:T(8,128)(2,1)S(1)}, bf16[16,4608]{1,0:T(8,128)(2,1)S(1)}, u32[]{:S(2)}, u32[]{:S(2)}) collective-permute-start(bf16[16,4608]{1,0:T(8,128)(2,1)S(1)} %pad_maximum_fusion.3), channel_id=1, source_target_pairs={{0,2},{1,3},{2,0},{3,1},{4,6},{5,7},{6,4},{7,5},{8,10},{9,11},{10,... | collective-permute-start | bytes 442376 | tf_op jit(solution)/shard_map/ppermute | solution.py:438
  12.3 12.9 %collective-permute-start.10 = (bf16[16,4608]{1,0:T(8,128)(2,1)S(1)}, bf16[16,4608]{1,0:T(8,128)(2,1)S(1)}, u32[]{:S(2)}, u32[]{:S(2)}) collective-permute-start(bf16[16,4608]{1,0:T(8,128)(2,1)S(1)} %pad_maximum_fusion.3), channel_id=1, source_target_pairs={{0,1},{1,0},{2,3},{3,2},{4,5},{5,4},{6,7},{7,6},{8,9},{9,8},{10,11... | collective-permute-start | bytes 442376 | tf_op jit(solution)/shard_map/ppermute | solution.py:438
  18.3 13.6 %collective-permute-start.6 = (bf16[64,1664]{1,0:T(8,128)(2,1)S(1)}, bf16[64,1664]{1,0:T(8,128)(2,1)}, u32[]{:S(2)}, u32[]{:S(2)}) collective-permute-start(bf16[64,1664]{1,0:T(8,128)(2,1)S(1)} %pad_maximum_fusion.2.refs_0_), channel_id=1, source_target_pairs={{0,4},{4,0},{8,12},{12,8},{16,20},{20,16},{24,28},{28,24},{1,5},{5... | collective-permute-start | bytes 638984 | tf_op jit(solution)/shard_map/ppermute | solution.py:438
  25.2 39.3 %collective-permute-start.15 = (bf16[64,4608]{1,0:T(8,128)(2,1)S(1)}, bf16[64,4608]{1,0:T(8,128)(2,1)S(1)}, u32[]{:S(2)}, u32[]{:S(2)}) collective-permute-start(bf16[64,4608]{1,0:T(8,128)(2,1)S(1)} %pad_maximum_fusion.refs_0_), channel_id=1, source_target_pairs={{0,24},{4,28},{8,16},{12,20},{16,8},{20,12},{24,0},{28,4},{1,25},{... | collective-permute-start | bytes 1769480 | tf_op jit(solution)/shard_map/ppermute | solution.py:438
  27.7 37.0 %collective-permute-start.14 = (bf16[64,4608]{1,0:T(8,128)(2,1)S(1)}, bf16[64,4608]{1,0:T(8,128)(2,1)}, u32[]{:S(2)}, u32[]{:S(2)}) collective-permute-start(bf16[64,4608]{1,0:T(8,128)(2,1)S(1)} %pad_maximum_fusion.refs_0_), channel_id=1, source_target_pairs={{0,16},{4,20},{8,24},{12,28},{16,0},{20,4},{24,8},{28,12},{1,17},{... | collective-permute-start | bytes 1769480 | tf_op jit(solution)/shard_map/ppermute | solution.py:438
  28.3 36.8 %collective-permute-start.13 = (bf16[64,4608]{1,0:T(8,128)(2,1)S(1)}, bf16[64,4608]{1,0:T(8,128)(2,1)}, u32[]{:S(2)}, u32[]{:S(2)}) collective-permute-start(bf16[64,4608]{1,0:T(8,128)(2,1)S(1)} %pad_maximum_fusion.refs_0_), channel_id=1, source_target_pairs={{0,8},{4,12},{8,0},{12,4},{16,24},{20,28},{24,16},{28,20},{1,9},{5... | collective-permute-start | bytes 1769480 | tf_op jit(solution)/shard_map/ppermute | solution.py:438
  28.8 29.3 %collective-permute-start.5 = (bf16[64,1664]{1,0:T(8,128)(2,1)S(1)}, bf16[64,1664]{1,0:T(8,128)(2,1)}, u32[]{:S(2)}, u32[]{:S(2)}) collective-permute-start(bf16[64,1664]{1,0:T(8,128)(2,1)S(1)} %pad_maximum_fusion.2.refs_0_), channel_id=1, source_target_pairs={{0,24},{4,28},{8,16},{12,20},{16,8},{20,12},{24,0},{28,4},{1,25},{... | collective-permute-start | bytes 638984 | tf_op jit(solution)/shard_map/ppermute | solution.py:438
  31.9 30.6 %collective-permute-start.4 = (bf16[64,1664]{1,0:T(8,128)(2,1)S(1)}, bf16[64,1664]{1,0:T(8,128)(2,1)}, u32[]{:S(2)}, u32[]{:S(2)}) collective-permute-start(bf16[64,1664]{1,0:T(8,128)(2,1)S(1)} %pad_maximum_fusion.2.refs_0_), channel_id=1, source_target_pairs={{0,16},{4,20},{8,24},{12,28},{16,0},{20,4},{24,8},{28,12},{1,17},{... | collective-permute-start | bytes 638984 | tf_op jit(solution)/shard_map/ppermute | solution.py:438
  58.1 5.8 collective-permute-start.3
  64.2 81.6 %collective-permute-start.16 = (bf16[64,4608]{1,0:T(8,128)(2,1)S(1)}, bf16[64,4608]{1,0:T(8,128)(2,1)}, u32[]{:S(2)}, u32[]{:S(2)}) collective-permute-start(bf16[64,4608]{1,0:T(8,128)(2,1)S(1)} %pad_maximum_fusion.refs_0_), channel_id=1, source_target_pairs={{0,4},{4,0},{8,12},{12,8},{16,20},{20,16},{24,28},{28,24},{1,5},{5... | collective-permute-start | bytes 1769480 | tf_op jit(solution)/shard_map/ppermute | solution.py:438
  64.5 81.2 %collective-permute-start.19 = (bf16[64,4608]{1,0:T(8,128)(2,1)S(1)}, bf16[64,4608]{1,0:T(8,128)(2,1)}, u32[]{:S(2)}, u32[]{:S(2)}) collective-permute-start(bf16[64,4608]{1,0:T(8,128)(2,1)S(1)} %collective-permute-done.15.refs_3_), channel_id=1, source_target_pairs={{0,4},{4,0},{8,12},{12,8},{16,20},{20,16},{24,28},{28,24},{1,5},{5... | collective-permute-start | bytes 1769480 | tf_op jit(solution)/shard_map/ppermute | solution.py:438
  64.7 81.1 %collective-permute-start.18 = (bf16[64,4608]{1,0:T(8,128)(2,1)}, bf16[64,4608]{1,0:T(8,128)(2,1)}, u32[]{:S(2)}, u32[]{:S(2)}) collective-permute-start(bf16[64,4608]{1,0:T(8,128)(2,1)} %collective-permute-done.14.refs_2_), channel_id=1, source_target_pairs={{0,4},{4,0},{8,12},{12,8},{16,20},{20,16},{24,28},{28,24},{1,5},{5... | collective-permute-start | bytes 1769480 | tf_op jit(solution)/shard_map/ppermute | solution.py:438
  65.1 80.7 %collective-permute-start.17 = (bf16[64,4608]{1,0:T(8,128)(2,1)}, bf16[64,4608]{1,0:T(8,128)(2,1)}, u32[]{:S(2)}, u32[]{:S(2)}) collective-permute-start(bf16[64,4608]{1,0:T(8,128)(2,1)} %collective-permute-done.13.refs_1_), channel_id=1, source_target_pairs={{0,4},{4,0},{8,12},{12,8},{16,20},{20,16},{24,28},{28,24},{1,5},{5... | collective-permute-start | bytes 1769480 | tf_op jit(solution)/shard_map/ppermute | solution.py:438
  397.3 54.3 %collective-permute-start.34 = (bf16[256,512]{1,0:T(8,128)(2,1)}, bf16[256,512]{1,0:T(8,128)(2,1)S(1)}, u32[]{:S(2)}, u32[]{:S(2)}) collective-permute-start(bf16[256,512]{1,0:T(8,128)(2,1)} %get-tuple-element.106), channel_id=1, source_target_pairs={{0,4},{4,0},{8,12},{12,8},{16,20},{20,16},{24,28},{28,24},{1,5},{5... | collective-permute-start | bytes 786440 | tf_op jit(solution)/shard_map/ppermute | solution.py:438
  406.4 123.1 %collective-permute-start.20 = (bf16[256,2048]{1,0:T(8,128)(2,1)}, bf16[256,2048]{1,0:T(8,128)(2,1)S(1)}, u32[]{:S(2)}, u32[]{:S(2)}) collective-permute-start(bf16[256,2048]{1,0:T(8,128)(2,1)} %get-tuple-element.96), channel_id=1, source_target_pairs={{0,4},{4,0},{8,12},{12,8},{16,20},{20,16},{24,28},{28,24},{1,5},{5... | collective-permute-start | bytes 3145736 | tf_op jit(solution)/shard_map/ppermute | solution.py:438
  442.4 36.2 %collective-permute-start.41 = (bf16[256,768]{1,0:T(8,128)(2,1)S(1)}, bf16[256,768]{1,0:T(8,128)(2,1)S(1)}, u32[]{:S(2)}, u32[]{:S(2)}) collective-permute-start(bf16[256,768]{1,0:T(8,128)(2,1)S(1)} %copy-done.24), channel_id=1, source_target_pairs={{0,4},{4,0},{8,12},{12,8},{16,20},{20,16},{24,28},{28,24},{1,5},{5... | collective-permute-start | bytes 1179656 | tf_op jit(solution)/shard_map/ppermute | solution.py:438
  451.7 10.2 %collective-permute-start.35 = (bf16[64,512]{1,0:T(8,128)(2,1)S(1)}, bf16[64,512]{1,0:T(8,128)(2,1)S(1)}, u32[]{:S(2)}, u32[]{:S(2)}) collective-permute-start(bf16[64,512]{1,0:T(8,128)(2,1)S(1)} %get-tuple-element.143), channel_id=1, source_target_pairs={{0,8},{4,12},{8,0},{12,4},{16,24},{20,28},{24,16},{28,20},{1,9},{5... | collective-permute-start | bytes 196616 | tf_op jit(solution)/shard_map/ppermute | solution.py:438
  453.2 8.6 %collective-permute-start.37 = (bf16[64,512]{1,0:T(8,128)(2,1)S(1)}, bf16[64,512]{1,0:T(8,128)(2,1)S(1)}, u32[]{:S(2)}, u32[]{:S(2)}) collective-permute-start(bf16[64,512]{1,0:T(8,128)(2,1)S(1)} %get-tuple-element.144), channel_id=1, source_target_pairs={{0,24},{4,28},{8,16},{12,20},{16,8},{20,12},{24,0},{28,4},{1,25},{... | collective-permute-start | bytes 196616 | tf_op jit(solution)/shard_map/ppermute | solution.py:438
  454.7 7.2 %collective-permute-start.36 = (bf16[64,512]{1,0:T(8,128)(2,1)S(1)}, bf16[64,512]{1,0:T(8,128)(2,1)S(1)}, u32[]{:S(2)}, u32[]{:S(2)}) collective-permute-start(bf16[64,512]{1,0:T(8,128)(2,1)S(1)} %get-tuple-element.145), channel_id=1, source_target_pairs={{0,16},{4,20},{8,24},{12,28},{16,0},{20,4},{24,8},{28,12},{1,17},{... | collective-permute-start | bytes 196616 | tf_op jit(solution)/shard_map/ppermute | solution.py:438
  476.5 5.8 collective-permute-start.48
  480.3 6.7 %collective-permute-start.44 = (bf16[64,768]{1,0:T(8,128)(2,1)S(1)}, bf16[64,768]{1,0:T(8,128)(2,1)S(1)}, u32[]{:S(2)}, u32[]{:S(2)}) collective-permute-start(bf16[64,768]{1,0:T(8,128)(2,1)S(1)} %get-tuple-element.141), channel_id=1, source_target_pairs={{0,24},{4,28},{8,16},{12,20},{16,8},{20,12},{24,0},{28,4},{1,25},{... | collective-permute-start | bytes 294920 | tf_op jit(solution)/shard_map/ppermute | solution.py:438
  481.8 6.6 %collective-permute-start.43 = (bf16[64,768]{1,0:T(8,128)(2,1)S(1)}, bf16[64,768]{1,0:T(8,128)(2,1)S(1)}, u32[]{:S(2)}, u32[]{:S(2)}) collective-permute-start(bf16[64,768]{1,0:T(8,128)(2,1)S(1)} %get-tuple-element.142), channel_id=1, source_target_pairs={{0,16},{4,20},{8,24},{12,28},{16,0},{20,4},{24,8},{28,12},{1,17},{... | collective-permute-start | bytes 294920 | tf_op jit(solution)/shard_map/ppermute | solution.py:438
  492.1 16.8 %collective-permute-start.49 = (bf16[64,896]{1,0:T(8,128)(2,1)S(1)}, bf16[64,896]{1,0:T(8,128)(2,1)S(1)}, u32[]{:S(2)}, u32[]{:S(2)}) collective-permute-start(bf16[64,896]{1,0:T(8,128)(2,1)S(1)} %get-tuple-element.137), channel_id=1, source_target_pairs={{0,8},{4,12},{8,0},{12,4},{16,24},{20,28},{24,16},{28,20},{1,9},{5... | collective-permute-start | bytes 344072 | tf_op jit(solution)/shard_map/ppermute | solution.py:438
  493.6 15.2 %collective-permute-start.51 = (bf16[64,896]{1,0:T(8,128)(2,1)S(1)}, bf16[64,896]{1,0:T(8,128)(2,1)S(1)}, u32[]{:S(2)}, u32[]{:S(2)}) collective-permute-start(bf16[64,896]{1,0:T(8,128)(2,1)S(1)} %get-tuple-element.138), channel_id=1, source_target_pairs={{0,24},{4,28},{8,16},{12,20},{16,8},{20,12},{24,0},{28,4},{1,25},{... | collective-permute-start | bytes 344072 | tf_op jit(solution)/shard_map/ppermute | solution.py:438
  508.8 7.8 %collective-permute-start.89 = (bf16[16,768]{1,0:T(8,128)(2,1)S(1)}, bf16[16,768]{1,0:T(8,128)(2,1)S(1)}, u32[]{:S(2)}, u32[]{:S(2)}) collective-permute-start(bf16[16,768]{1,0:T(8,128)(2,1)S(1)} %collective-permute-done.88), channel_id=1, source_target_pairs={{0,4},{4,0},{8,12},{12,8},{16,20},{20,16},{24,28},{28,24},{1,5},{5... | collective-permute-start | bytes 73736 | tf_op jit(solution)/shard_map/ppermute | solution.py:438
  525.3 8.3 %collective-permute-start.27 = (bf16[256,2048]{1,0:T(8,128)(2,1)S(1)}, bf16[256,2048]{1,0:T(8,128)(2,1)S(1)}, u32[]{:S(2)}, u32[]{:S(2)}) collective-permute-start(bf16[256,2048]{1,0:T(8,128)(2,1)S(1)} %copy-done.23), channel_id=1, source_target_pairs={{0,4},{4,0},{8,12},{12,8},{16,20},{20,16},{24,28},{28,24},{1,5},{5... | collective-permute-start | bytes 3145736 | tf_op jit(solution)/shard_map/ppermute | solution.py:438
  530.0 9.2 %collective-permute-start.21 = (bf16[64,2048]{1,0:T(8,128)(2,1)S(1)}, bf16[64,2048]{1,0:T(8,128)(2,1)S(1)}, u32[]{:S(2)}, u32[]{:S(2)}) collective-permute-start(bf16[64,2048]{1,0:T(8,128)(2,1)S(1)} %get-tuple-element.134), channel_id=1, source_target_pairs={{0,8},{4,12},{8,0},{12,4},{16,24},{20,28},{24,16},{28,20},{1,9},{5... | collective-permute-start | bytes 786440 | tf_op jit(solution)/shard_map/ppermute | solution.py:438
  531.0 14.2 %collective-permute-start.23 = (bf16[64,2048]{1,0:T(8,128)(2,1)S(1)}, bf16[64,2048]{1,0:T(8,128)(2,1)S(1)}, u32[]{:S(2)}, u32[]{:S(2)}) collective-permute-start(bf16[64,2048]{1,0:T(8,128)(2,1)S(1)} %get-tuple-element.135), channel_id=1, source_target_pairs={{0,24},{4,28},{8,16},{12,20},{16,8},{20,12},{24,0},{28,4},{1,25},{... | collective-permute-start | bytes 786440 | tf_op jit(solution)/shard_map/ppermute | solution.py:438
  532.4 14.7 %collective-permute-start.22 = (bf16[64,2048]{1,0:T(8,128)(2,1)S(1)}, bf16[64,2048]{1,0:T(8,128)(2,1)S(1)}, u32[]{:S(2)}, u32[]{:S(2)}) collective-permute-start(bf16[64,2048]{1,0:T(8,128)(2,1)S(1)} %get-tuple-element.136), channel_id=1, source_target_pairs={{0,16},{4,20},{8,24},{12,28},{16,0},{20,4},{24,8},{28,12},{1,17},{... | collective-permute-start | bytes 786440 | tf_op jit(solution)/shard_map/ppermute | solution.py:438
  534.1 16.4 %collective-permute-start.28 = (bf16[64,2048]{1,0:T(8,128)(2,1)S(1)}, bf16[64,2048]{1,0:T(8,128)(2,1)S(1)}, u32[]{:S(2)}, u32[]{:S(2)}) collective-permute-start(bf16[64,2048]{1,0:T(8,128)(2,1)S(1)} %get-tuple-element.131), channel_id=1, source_target_pairs={{0,8},{4,12},{8,0},{12,4},{16,24},{20,28},{24,16},{28,20},{1,9},{5... | collective-permute-start | bytes 786440 | tf_op jit(solution)/shard_map/ppermute | solution.py:438
  535.0 20.7 %collective-permute-start.30 = (bf16[64,2048]{1,0:T(8,128)(2,1)S(1)}, bf16[64,2048]{1,0:T(8,128)(2,1)S(1)}, u32[]{:S(2)}, u32[]{:S(2)}) collective-permute-start(bf16[64,2048]{1,0:T(8,128)(2,1)S(1)} %get-tuple-element.132), channel_id=1, source_target_pairs={{0,24},{4,28},{8,16},{12,20},{16,8},{20,12},{24,0},{28,4},{1,25},{... | collective-permute-start | bytes 786440 | tf_op jit(solution)/shard_map/ppermute | solution.py:438
  539.2 17.8 %collective-permute-start.29 = (bf16[64,2048]{1,0:T(8,128)(2,1)S(1)}, bf16[64,2048]{1,0:T(8,128)(2,1)S(1)}, u32[]{:S(2)}, u32[]{:S(2)}) collective-permute-start(bf16[64,2048]{1,0:T(8,128)(2,1)S(1)} %get-tuple-element.133), channel_id=1, source_target_pairs={{0,16},{4,20},{8,24},{12,28},{16,0},{20,4},{24,8},{28,12},{1,17},{... | collective-permute-start | bytes 786440 | tf_op jit(solution)/shard_map/ppermute | solution.py:438
  547.3 12.7 %collective-permute-start.24 = (bf16[16,2048]{1,0:T(8,128)(2,1)S(1)}, bf16[16,2048]{1,0:T(8,128)(2,1)S(1)}, u32[]{:S(2)}, u32[]{:S(2)}) collective-permute-start(bf16[16,2048]{1,0:T(8,128)(2,1)S(1)} %get-tuple-element.149), channel_id=1, source_target_pairs={{0,1},{1,0},{2,3},{3,2},{4,5},{5,4},{6,7},{7,6},{8,9},{9,8},{10,11... | collective-permute-start | bytes 196616 | tf_op jit(solution)/shard_map/ppermute | solution.py:438
  548.1 12.7 %collective-permute-start.26 = (bf16[16,2048]{1,0:T(8,128)(2,1)S(1)}, bf16[16,2048]{1,0:T(8,128)(2,1)S(1)}, u32[]{:S(2)}, u32[]{:S(2)}) collective-permute-start(bf16[16,2048]{1,0:T(8,128)(2,1)S(1)} %get-tuple-element.150), channel_id=1, source_target_pairs={{0,3},{1,2},{2,1},{3,0},{4,7},{5,6},{6,5},{7,4},{8,11},{9,10},{10,... | collective-permute-start | bytes 196616 | tf_op jit(solution)/shard_map/ppermute | solution.py:438
  550.5 10.3 %collective-permute-start.25 = (bf16[16,2048]{1,0:T(8,128)(2,1)S(1)}, bf16[16,2048]{1,0:T(8,128)(2,1)S(1)}, u32[]{:S(2)}, u32[]{:S(2)}) collective-permute-start(bf16[16,2048]{1,0:T(8,128)(2,1)S(1)} %get-tuple-element.151), channel_id=1, source_target_pairs={{0,2},{1,3},{2,0},{3,1},{4,6},{5,7},{6,4},{7,5},{8,10},{9,11},{10,... | collective-permute-start | bytes 196616 | tf_op jit(solution)/shard_map/ppermute | solution.py:438
  557.2 7.2 %collective-permute-start.31 = (bf16[16,2048]{1,0:T(8,128)(2,1)S(1)}, bf16[16,2048]{1,0:T(8,128)(2,1)S(1)}, u32[]{:S(2)}, u32[]{:S(2)}) collective-permute-start(bf16[16,2048]{1,0:T(8,128)(2,1)S(1)} %get-tuple-element.146), channel_id=1, source_target_pairs={{0,1},{1,0},{2,3},{3,2},{4,5},{5,4},{6,7},{7,6},{8,9},{9,8},{10,11... | collective-permute-start | bytes 196616 | tf_op jit(solution)/shard_map/ppermute | solution.py:438
  558.1 6.9 %collective-permute-start.33 = (bf16[16,2048]{1,0:T(8,128)(2,1)S(1)}, bf16[16,2048]{1,0:T(8,128)(2,1)S(1)}, u32[]{:S(2)}, u32[]{:S(2)}) collective-permute-start(bf16[16,2048]{1,0:T(8,128)(2,1)S(1)} %get-tuple-element.147), channel_id=1, source_target_pairs={{0,3},{1,2},{2,1},{3,0},{4,7},{5,6},{6,5},{7,4},{8,11},{9,10},{10,... | collective-permute-start | bytes 196616 | tf_op jit(solution)/shard_map/ppermute | solution.py:438
  559.9 6.4 %collective-permute-start.32 = (bf16[16,2048]{1,0:T(8,128)(2,1)S(1)}, bf16[16,2048]{1,0:T(8,128)(2,1)S(1)}, u32[]{:S(2)}, u32[]{:S(2)}) collective-permute-start(bf16[16,2048]{1,0:T(8,128)(2,1)S(1)} %get-tuple-element.148), channel_id=1, source_target_pairs={{0,2},{1,3},{2,0},{3,1},{4,6},{5,7},{6,4},{7,5},{8,10},{9,11},{10,... | collective-permute-start | bytes 196616 | tf_op jit(solution)/shard_map/ppermute | solution.py:438
  560.8 47.1 %collective-permute-start.67 = (bf16[16,2048]{1,0:T(8,128)(2,1)S(1)}, bf16[16,2048]{1,0:T(8,128)(2,1)S(1)}, u32[]{:S(2)}, u32[]{:S(2)}) collective-permute-start(bf16[16,2048]{1,0:T(8,128)(2,1)S(1)} %get-tuple-element.130), channel_id=1, source_target_pairs={{0,24},{4,28},{8,16},{12,20},{16,8},{20,12},{24,0},{28,4},{1,25},{... | collective-permute-start | bytes 196616 | tf_op jit(solution)/shard_map/ppermute | solution.py:438
  562.4 46.1 %collective-permute-start.65 = (bf16[16,2048]{1,0:T(8,128)(2,1)S(1)}, bf16[16,2048]{1,0:T(8,128)(2,1)S(1)}, u32[]{:S(2)}, u32[]{:S(2)}) collective-permute-start(bf16[16,2048]{1,0:T(8,128)(2,1)S(1)} %get-tuple-element.130), channel_id=1, source_target_pairs={{0,16},{4,20},{8,24},{12,28},{16,0},{20,4},{24,8},{28,12},{1,17},{... | collective-permute-start | bytes 196616 | tf_op jit(solution)/shard_map/ppermute | solution.py:438
  564.3 37.9 %collective-permute-start.63 = (bf16[16,2048]{1,0:T(8,128)(2,1)S(1)}, bf16[16,2048]{1,0:T(8,128)(2,1)S(1)}, u32[]{:S(2)}, u32[]{:S(2)}) collective-permute-start(bf16[16,2048]{1,0:T(8,128)(2,1)S(1)} %get-tuple-element.130), channel_id=1, source_target_pairs={{0,8},{4,12},{8,0},{12,4},{16,24},{20,28},{24,16},{28,20},{1,9},{5... | collective-permute-start | bytes 196616 | tf_op jit(solution)/shard_map/ppermute | solution.py:438
  565.0 36.3 %collective-permute-start.62 = (bf16[16,2048]{1,0:T(8,128)(2,1)S(1)}, bf16[16,2048]{1,0:T(8,128)(2,1)S(1)}, u32[]{:S(2)}, u32[]{:S(2)}) collective-permute-start(bf16[16,2048]{1,0:T(8,128)(2,1)S(1)} %get-tuple-element.130), channel_id=1, source_target_pairs={{0,4},{4,0},{8,12},{12,8},{16,20},{20,16},{24,28},{28,24},{1,5},{5... | collective-permute-start | bytes 196616 | tf_op jit(solution)/shard_map/ppermute | solution.py:438
  599.1 9.5 %collective-permute-start.74 = (bf16[16,2048]{1,0:T(8,128)(2,1)S(1)}, bf16[16,2048]{1,0:T(8,128)(2,1)S(1)}, u32[]{:S(2)}, u32[]{:S(2)}) collective-permute-start(bf16[16,2048]{1,0:T(8,128)(2,1)S(1)} %get-tuple-element.128), channel_id=1, source_target_pairs={{0,24},{4,28},{8,16},{12,20},{16,8},{20,12},{24,0},{28,4},{1,25},{... | collective-permute-start | bytes 196616 | tf_op jit(solution)/shard_map/ppermute | solution.py:438
  601.3 7.7 %collective-permute-start.72 = (bf16[16,2048]{1,0:T(8,128)(2,1)S(1)}, bf16[16,2048]{1,0:T(8,128)(2,1)S(1)}, u32[]{:S(2)}, u32[]{:S(2)}) collective-permute-start(bf16[16,2048]{1,0:T(8,128)(2,1)S(1)} %get-tuple-element.128), channel_id=1, source_target_pairs={{0,16},{4,20},{8,24},{12,28},{16,0},{20,4},{24,8},{28,12},{1,17},{... | collective-permute-start | bytes 196616 | tf_op jit(solution)/shard_map/ppermute | solution.py:438
  (74 other events, 693.5 us)
